TPU v7x, 32 devices: a whole 2x2x4 slice. The times are simulated.
32 devices in a mesh: dp: 32 (over z, y, x, core).
Axes of the slice: x: 2, y: 2, z: 4, core: 2. Of those that a mesh axis runs over, the one named last changes fastest.
Arguments:
- queries: bfloat16 [4096, 768], P('dp'), may hold values from -2 to 2
- documents: bfloat16 [4096, 768], P('dp'), may hold values from -2 to 2
- positives: int32 [4096], P('dp'), may hold values from 0 to 4095, each once
Outputs:
- loss: float32 [], replicated
- grad_queries: float32 [4096, 768], P('dp')
- grad_documents: float32 [4096, 768], P('dp')
Inputs may be any that keep to these rules, and one draw needn't show every extreme that they name: `positives`: every document is the positive of exactly one query.
All inputs are finite; a program needn't handle non-finite values.
Results may differ from a plain program's by a relative error of at most 0.0004.
The roundings to bfloat16 on the way count: a program that leaves them out, or rounds other values in their place, can miss the bound.
Values may be sent and summed in bfloat16 or wider, within the bound.
A program may use at most 192 MiB of HBM per device.

v0:
```python
import math

import jax
import jax.numpy as jnp
from jax import lax
from jax.sharding import PartitionSpec as P


def normalize(values):
    wide = values.astype(jnp.float32)
    length = jnp.sqrt(jnp.sum(wide * wide, axis=1, keepdims=True) + 1e-06)
    return (wide / length, length)


def contract_rows(left, right):
    return lax.dot_general(
        left, right, (((0,), (0,)), ((), ())), preferred_element_type=jnp.float32
    )


def contract_cols(left, right):
    return lax.dot_general(
        left, right, (((1,), (1,)), ((), ())), preferred_element_type=jnp.float32
    )


def local(queries, documents, positives):
    qn, qnorm = normalize(queries)
    dn, dnorm = normalize(documents)
    qb = qn.astype(jnp.bfloat16)
    db = dn.astype(jnp.bfloat16)
    count_q, width = qb.shape
    alldocs = lax.all_gather(db, "dp", axis=0, tiled=True)
    count_docs = alldocs.shape[0]
    block = math.gcd(count_docs, 1024)
    nblocks = count_docs // block
    blocks = alldocs.reshape(nblocks, block, width)
    starts = lax.iota(jnp.int32, nblocks) * block

    def add_total(total, rows):
        scores = 20.0 * contract_cols(qb, rows)
        return (total + jnp.sum(jnp.exp(scores - 20.0), axis=1), None)

    total, unused = lax.scan(add_total, jnp.zeros((count_q,), jnp.float32), blocks)
    lse = 20.0 + jnp.log(total)
    picked = jnp.take(alldocs, positives, axis=0)
    positive_score = 20.0 * jnp.sum(qb.astype(jnp.float32) * picked.astype(jnp.float32), axis=1)
    loss_sum = lax.psum(jnp.sum(lse - positive_score), "dp")
    loss = loss_sum / (count_q * lax.axis_size("dp"))

    def weights_of(rows, start):
        scores = 20.0 * contract_cols(qb, rows)
        columns = start + lax.iota(jnp.int32, rows.shape[0])
        hit = (positives[:, None] == columns[None, :]).astype(jnp.float32)
        return (jnp.exp(scores - lse[:, None]) - hit).astype(jnp.bfloat16)

    def add_grad(acc, item):
        rows, start = item
        weights = weights_of(rows, start)
        acc = acc + 20.0 * jnp.dot(weights, rows, preferred_element_type=jnp.float32)
        return (acc, None)

    gq, stacked = lax.scan(add_grad, jnp.zeros((count_q, width), jnp.float32), (blocks, starts))
    grad_queries = (gq - jnp.sum(gq * qn, axis=1, keepdims=True) * qn) / qnorm
    rows = alldocs
    gd = lax.psum_scatter(
        20.0 * contract_rows(weights_of(rows, jnp.int32(0)), qb),
        "dp",
        scatter_dimension=0,
        tiled=True,
    )
    grad_documents = (gd - jnp.sum(gd * dn, axis=1, keepdims=True) * dn) / dnorm
    return (loss, grad_queries, grad_documents)


def solution(mesh):
    placed = (P("dp", None), P("dp", None), P("dp"))
    return jax.shard_map(
        local,
        mesh=mesh,
        in_specs=placed,
        out_specs=(P(), P("dp", None), P("dp", None)),
        check_vma=False,
    )
```

profile of v0, /device:TPU:0, one launch (start us, length us, event | category | flops | bytes accessed | tf_op | source)
XLA Modules:
  0.0 275.0 jit_solution(943378032617575929)
XLA Ops:
  7.2 0.0 all-gather.2.cloned.1.call-start
  7.2 1.0 fusion.65
  8.3 1.7 fusion.68
  10.0 0.0 all-gather.2.cloned.1.call-update
  10.0 0.0 reduce-scatter.2.cloned.1.call-start
  10.1 0.7 compare_select_fusion
  10.7 1.0 fusion.66
  11.8 0.7 compare_and_fusion
  12.5 71.2 %all-gather.2.cloned.1.call-done = bf16[4096,768]{1,0:T(8,128)(2,1)} async-done(((bf16[128,768]{1,0:T(8,128)(2,1)}), bf16[4096,768]{1,0:T(8,128)(2,1)}) %all-gather.2.cloned.1.call-update) | async-done | bytes 6291472 | tf_op jit(solution)/shard_map/all_gather | solution.py:33
  83.7 4.6 %gather_fusion = bf16[128,768]{1,0:T(8,128)(2,1)S(1)} fusion(bf16[4096,768]{1,0:T(8,128)(2,1)} %all-gather.2.cloned.1.call-done, s32[1024]{0:T(1024)S(1)} %pad_clamp_fusion), kind=kCustom, calls=%fused_computation | custom fusion | bytes 393728 | tf_op jit(solution)/shard_map/jit(_take)/gather | solution.py:46
  88.2 0.0 copy-start.2
  88.3 1.2 multiply_reduce_fusion.2
  89.4 8.1 %while.24 = (s32[]{:T(128)}, f32[128]{0:T(128)S(1)}, bf16[4,1024,768]{2,1,0:T(8,128)(2,1)}, bf16[128,768]{1,0:T(8,128)(2,1)S(1)}, s32[]{:T(128)}, /*index=5*/s32[]{:T(128)}) while((s32[]{:T(128)}, f32[128]{0:T(128)S(1)}, bf16[4,1024,768]{2,1,0:T(8,128)(2,1)}, bf16[128,768]{1,0:T(8,128)(2,1)S(1)}, s32[]{:T(128)}, ...), condition=%wide.region_4.5_spmd.clone, body=%wide.region_2.4_spmd.clone.sunk | while | flops 201719936 | bytes 1771611 | solution.py:44
  89.4 2.0 fusion.86
  91.5 2.0 fusion.86
  93.5 2.0 fusion.86
  95.5 2.0 fusion.86
  97.6 0.6 log_add_fusion
  98.2 0.0 copy-done.2
  98.2 11.2 %convolution_multiply_fusion = f32[4096,768]{1,0:T(8,128)} fusion(bf16[128,768]{1,0:T(8,128)(2,1)S(1)} %get-tuple-element.279, bf16[4096,768]{1,0:T(8,128)(2,1)} %bitcast.64, s32[128]{0:T(128)S(1)} %copy-done.2, f32[128]{0:T(128)S(1)} %get-tuple-element.250), kind=kOutput, calls=%fused_computation.34 | convolution fusion | flops 1616904192 | bytes 19072000 | tf_op jit(solution)/shard_map/dot_general | solution.py:16
  109.4 0.0 reduce-scatter.2.cloned.1.call-update
  109.4 39.5 %psum.7 = f32[]{:T(128)} all-reduce(f32[]{:T(128)} %get-tuple-element.159), channel_id=1, replica_groups=mesh['dp'=32] {'dp'}, use_global_device_ids=true, to_apply=%region_7.8 | all-reduce | flops 1 | bytes 8 | tf_op jit(solution)/shard_map/psum | solution.py:48
  149.6 0.0 copy-start.1
  149.6 0.0 copy-start
  149.6 17.8 %while.25 = (s32[]{:T(128)}, f32[128,768]{1,0:T(8,128)S(1)}, bf16[4,1024,768]{2,1,0:T(8,128)(2,1)}, bf16[128,768]{1,0:T(8,128)(2,1)S(1)}, f32[128]{0:T(128)S(1)}...) while((s32[]{:T(128)}, f32[128,768]{1,0:T(8,128)S(1)}, ...), condition=%wide.region_9.10_spmd.clone, body=%wide.region_8.9_spmd.clone.sunk | while | flops 403735552 | bytes 4139646 | solution.py:63
  149.6 0.6 dynamic_slice.62
  150.2 0.7 iota_add_fusion.2
  150.9 3.3 %fusion.91 = f32[128,768]{1,0:T(8,128)S(1)} fusion(bf16[4,1024,768]{2,1,0:T(8,128)(2,1)} %get-tuple-element.266, s32[]{:T(128)S(6)} %copy.14, bf16[128,768]{1,0:T(8,128)(2,1)S(1)} %get-tuple-element.267, f32[128,768]{1,0:T(8,128)S(1)} %get-tuple-element.256, s32[128]{0:T(128)S(1)} %get-tuple-element.269, f32[128]{0:T(128)S(1)} %get-tuple-element.268, ...), kind=kOutput, calls=%fused_computation.24.clone.1 | convolution fusion | flops 403734528 | bytes 4135424 | tf_op jit(solution)/shard_map/while/body/eval_jaxpr/dot_general | solution.py:60
  154.2 0.6 dynamic_slice.62
  154.8 0.6 iota_add_fusion.2
  155.5 3.1 %fusion.91 = f32[128,768]{1,0:T(8,128)S(1)} fusion(bf16[4,1024,768]{2,1,0:T(8,128)(2,1)} %get-tuple-element.266, s32[]{:T(128)S(6)} %copy.14, bf16[128,768]{1,0:T(8,128)(2,1)S(1)} %get-tuple-element.267, f32[128,768]{1,0:T(8,128)S(1)} %get-tuple-element.256, s32[128]{0:T(128)S(1)} %get-tuple-element.269, f32[128]{0:T(128)S(1)} %get-tuple-element.268, ...), kind=kOutput, calls=%fused_computation.24.clone.1 | convolution fusion | flops 403734528 | bytes 4135424 | tf_op jit(solution)/shard_map/while/body/eval_jaxpr/dot_general | solution.py:60
  158.6 0.6 dynamic_slice.62
  159.2 0.6 iota_add_fusion.2
  159.8 3.1 %fusion.91 = f32[128,768]{1,0:T(8,128)S(1)} fusion(bf16[4,1024,768]{2,1,0:T(8,128)(2,1)} %get-tuple-element.266, s32[]{:T(128)S(6)} %copy.14, bf16[128,768]{1,0:T(8,128)(2,1)S(1)} %get-tuple-element.267, f32[128,768]{1,0:T(8,128)S(1)} %get-tuple-element.256, s32[128]{0:T(128)S(1)} %get-tuple-element.269, f32[128]{0:T(128)S(1)} %get-tuple-element.268, ...), kind=kOutput, calls=%fused_computation.24.clone.1 | convolution fusion | flops 403734528 | bytes 4135424 | tf_op jit(solution)/shard_map/while/body/eval_jaxpr/dot_general | solution.py:60
  163.0 0.6 dynamic_slice.62
  163.6 0.7 iota_add_fusion.2
  164.2 3.2 %fusion.91 = f32[128,768]{1,0:T(8,128)S(1)} fusion(bf16[4,1024,768]{2,1,0:T(8,128)(2,1)} %get-tuple-element.266, s32[]{:T(128)S(6)} %copy.14, bf16[128,768]{1,0:T(8,128)(2,1)S(1)} %get-tuple-element.267, f32[128,768]{1,0:T(8,128)S(1)} %get-tuple-element.256, s32[128]{0:T(128)S(1)} %get-tuple-element.269, f32[128]{0:T(128)S(1)} %get-tuple-element.268, ...), kind=kOutput, calls=%fused_computation.24.clone.1 | convolution fusion | flops 403734528 | bytes 4135424 | tf_op jit(solution)/shard_map/while/body/eval_jaxpr/dot_general | solution.py:60
  167.5 0.0 copy-done.1
  167.5 0.2 multiply_reduce_fusion.1
  167.7 0.9 subtract_divide_fusion.1
  168.6 95.4 %reduce-scatter.2.cloned.1.call-done = f32[128,768]{1,0:T(8,128)} async-done(((f32[4096,768]{1,0:T(8,128)}), f32[128,768]{1,0:T(8,128)}) %reduce-scatter.2.cloned.1.call-update) | async-done | bytes 393232 | tf_op jit(solution)/shard_map/reduce_scatter | solution.py:66
  263.9 0.0 copy-done
  263.9 1.2 multiply_reduce_fusion
  265.1 1.9 subtract_divide_fusion
  (10 shorter events, 0.1 us)
Async XLA Ops:
  7.2 76.5 %all-gather.2.cloned.1.call-start = ((), (), s32[]{:S(2)}) async-start(), calls=%async_computation.1 | async-start | bytes 6488064 | tf_op jit(solution)/shard_map/all_gather | solution.py:33
  10.0 253.9 %reduce-scatter.2.cloned.1.call-start = ((), (), s32[]{:S(2)}) async-start(), calls=%async_computation.2 | async-start | bytes 12976128 | tf_op jit(solution)/shard_map/reduce_scatter | solution.py:66
  88.2 9.9 %copy-start.2 = (s32[128]{0:T(128)S(1)}, s32[128]{0:T(128)}, u32[]{:S(2)}) copy-start(s32[128]{0:T(128)} %param.9) | copy-start | bytes 1540
  149.6 17.8 %copy-start.1 = (bf16[128,768]{1,0:T(8,128)(2,1)S(1)}, bf16[128,768]{1,0:T(8,128)(2,1)}, u32[]{:S(2)}) copy-start(bf16[128,768]{1,0:T(8,128)(2,1)} %param.7) | copy-start | bytes 589828
  149.6 114.3 %copy-start = (bf16[128,768]{1,0:T(8,128)(2,1)S(1)}, bf16[128,768]{1,0:T(8,128)(2,1)}, u32[]{:S(2)}) copy-start(bf16[128,768]{1,0:T(8,128)(2,1)} %param.8) | copy-start | bytes 589828
Sparse Core Ops, SparseCore 0:
  11.4 72.1 all-gather.1
  109.5 154.3 reduce-scatter.1
where the time goes:
time: 276 us; the launch traced here: 275 us
  waiting for transfers between devices  167 us (61%)
  blocking collectives  39.5 us (14%)
  matrix products  31.9 us (12%)
  between operations  15.9 us (6%)
  other arithmetic  13.8 us (5%)
  local copies, waits for them, and re-layouts  6.92 us (3%)
    reduce_scatter x1, waiting for transfers between devices, local(): lax.psum_scatter(20.0 * contract_rows(weights_of(rows, jnp.int32(0)), qb)...  95.4 us
    all_gather x1, waiting for transfers between devices, local(): alldocs = lax.all_gather(db, 'dp', axis=0, tiled=True)  71.2 us
    psum x1, blocking collectives, local(): loss_sum = lax.psum(jnp.sum(lse - positive_score), 'dp')  39.5 us
    dot_general x4, matrix products, add_grad(): jnp.dot(weights, rows, preferred_element_type=jnp.float32)  12.7 us
    dot_general x1, matrix products, contract_rows(): lax.dot_general(left, right, (((0,), (0,)), ((), ())), preferred_element_...  11.2 us
    dot_general x4, matrix products, contract_cols(): lax.dot_general(left, right, (((1,), (1,)), ((), ())), preferred_element_...  8.01 us
  transfers between devices with their start and end apart: 2, of which 2 were waited for; matrix products, arithmetic and copies ran while one was open for 8% of the time, Pallas kernels for 0%

commit v1 on v0

v1 whole, which is shorter than its diff:
```python
import functools

import jax
import jax.numpy as jnp
from jax import lax
from jax.experimental import pallas as pl
from jax.experimental.pallas import tpu as pltpu
from jax.sharding import PartitionSpec as P

PIECES = 2
F32 = jnp.float32
BF16 = jnp.bfloat16


def tree_sum(terms):
    while len(terms) > 1:
        terms = [terms[i] + terms[i + 1] for i in range(0, len(terms), 2)]
    return terms[0]


def normalize(values):
    wide = values.astype(F32)
    length = jnp.sqrt(jnp.sum(wide * wide, axis=1, keepdims=True) + 1e-06)
    return wide / length, length


def project(grad, unit, length):
    return (grad - jnp.sum(grad * unit, axis=1, keepdims=True) * unit) / length


def group_bits(n):
    bits = n.bit_length() - 1
    odd = [b for b in range(bits - 1, 0, -1) if b % 2 == 1]
    even = [b for b in range(bits - 1, 0, -1) if b % 2 == 0]
    return odd + [0], even


def kernel(
    n, qbits, dbits,
    q_ref, d_ref, pos_ref,
    loss_ref, outq_ref, outd_ref,
    qall, dall, posrow, expd, wts, stats, losses, accq, accd, gotq, gotd,
    qs_sem, qr_sem, ds_sem, dr_sem, ps_sem, pr_sem, ss_sem, sr_sem, ls_sem, lr_sem,
    aqs_sem, aqr_sem, ads_sem, adr_sem,
):
    me = lax.axis_index("dp")
    c = q_ref.shape[0]
    piece = c // PIECES
    nq, nd = 1 << len(qbits), 1 << len(dbits)
    rows_q, rows_d = nq * c, nd * c

    def flipped(bits, slot):
        where = me
        for j, b in enumerate(bits):
            if (slot >> j) & 1:
                where = where + (1 - 2 * (lax.rem(lax.div(me, 1 << b), 2))) * (1 << b)
        return where

    peer_q = [flipped(qbits, k) for k in range(nq)]
    peer_d = [flipped(dbits, k) for k in range(nd)]

    barrier = pltpu.get_barrier_semaphore()
    for peer in peer_q[1:] + peer_d[1:]:
        pl.semaphore_signal(barrier, inc=1, device_id=(peer,), device_id_type=pl.DeviceIdType.MESH)

    qn, qnorm = normalize(q_ref[...])
    dn, dnorm = normalize(d_ref[...])
    qall[pl.ds(0, c), :] = qn.astype(BF16)
    dall[pl.ds(0, c), :] = dn.astype(BF16)
    posrow[:, pl.ds(0, c)] = pos_ref[...]

    pl.semaphore_wait(barrier, nq + nd - 2)

    def remote(src, dst, send, recv, peer):
        return pltpu.make_async_remote_copy(
            src_ref=src, dst_ref=dst, send_sem=send, recv_sem=recv,
            device_id=(peer,), device_id_type=pl.DeviceIdType.MESH,
        )

    def stage_of(slot):
        return slot.bit_length() - 1

    def gather_copy(buf, send, recv, peers, slot, p):
        low = slot - (1 << stage_of(slot))
        return remote(
            buf.at[pl.ds(low * c + p * piece, piece), :],
            buf.at[pl.ds(slot * c + p * piece, piece), :],
            send.at[slot, p], recv.at[slot, p], peers[1 << stage_of(slot)],
        )

    gq = functools.partial(gather_copy, qall, qs_sem, qr_sem, peer_q)
    gd = functools.partial(gather_copy, dall, ds_sem, dr_sem, peer_d)
    pos_copies = [
        remote(posrow.at[:, pl.ds(0, c)], posrow.at[:, pl.ds(k * c, c)],
               ps_sem.at[k], pr_sem.at[k], peer_q[k])
        for k in range(1, nq)
    ]

    for p in range(PIECES):
        for j in range(max(len(qbits), len(dbits))):
            if j < len(dbits):
                gd(1 << j, p).start()
            if j < len(qbits):
                gq(1 << j, p).start()
    for copy in pos_copies:
        copy.start()

    def arrive(make, bits, slot, p):
        make(slot, p).wait_recv()
        for j in range(stage_of(slot) + 1, len(bits)):
            make(slot + (1 << j), p).start()

    half = nq // 2
    for slot in range(1, max(half, nd)):
        for p in range(PIECES):
            if slot < half:
                arrive(gq, qbits, slot, p)
            if slot < nd:
                arrive(gd, dbits, slot, p)
    for copy in pos_copies:
        copy.wait_recv()

    pair = 2 * c
    bases = [peer_d[r] * c for r in range(nd)]

    def hits(j, r):
        here = posrow[:, pl.ds(pl.multiple_of(j * pair, pair), pair)] - bases[r]
        return lax.broadcasted_iota(jnp.int32, (c, pair), 0) == here

    def score_pair(j, carry):
        lanes = pl.ds(pl.multiple_of(j * pair, pair), pair)
        total = jnp.zeros((1, pair), F32)
        picked = jnp.zeros((1, pair), F32)
        dots = lax.dot_general(
            dall[...], qall[lanes, :], (((1,), (1,)), ((), ())), preferred_element_type=F32
        )
        for r in range(nd):
            scores = 20.0 * dots[r * c:(r + 1) * c, :]
            powers = jnp.exp(scores - 20.0)
            expd[pl.ds(r * c, c), lanes] = powers
            total = total + jnp.sum(powers, axis=0, keepdims=True)
            picked = picked + jnp.sum(jnp.where(hits(j, r), scores, 0.0), axis=0, keepdims=True)
        stats[0, 0:1, lanes] = total
        stats[0, 1:2, lanes] = picked
        return carry

    lax.fori_loop(0, nq // 4, score_pair, 0)
    for slot in range(half, nq):
        for p in range(PIECES):
            gq(slot, p).wait_recv()
    lax.fori_loop(nq // 4, nq // 2, score_pair, 0)

    stat_copies = [
        remote(stats.at[0], stats.at[k], ss_sem.at[k], sr_sem.at[k], peer_q[k])
        for k in range(1, nq)
    ]
    for copy in stat_copies:
        copy.start()
    for copy in stat_copies:
        copy.wait_recv()

    def slot_total(row, r):
        return tree_sum([stats[k, row:row + 1, pl.ds((r ^ k) * c, c)] for k in range(nq)])

    totals = [slot_total(0, r) for r in range(nq)]
    losses[0] = tree_sum([20.0 + jnp.log(totals[r]) - slot_total(1, r) for r in range(nq)])
    loss_copies = [
        remote(losses.at[0], losses.at[k], ls_sem.at[k], lr_sem.at[k], peer_d[k])
        for k in range(1, nd)
    ]

    for j in range(nq // 2):
        inverse = 1.0 / jnp.concatenate([totals[2 * j], totals[2 * j + 1]], axis=1)
        lanes = pl.ds(j * pair, pair)
        for r in range(nd):
            rows = pl.ds(r * c, c)
            hit = jnp.where(hits(j, r), 1.0, 0.0)
            wts[rows, lanes] = (expd[rows, lanes] * inverse - hit).astype(BF16)

    def reduce_copy(acc, got, send, recv, peers, slot, p):
        rows = pl.ds(slot * c + p * piece, piece)
        return remote(acc.at[rows, :], got.at[rows, :], send.at[slot, p], recv.at[slot, p],
                      peers[1 << stage_of(slot)])

    rq = functools.partial(reduce_copy, accq, gotq, aqs_sem, aqr_sem, peer_q)
    rd = functools.partial(reduce_copy, accd, gotd, ads_sem, adr_sem, peer_d)

    def grad_q(j):
        rows = pl.ds(j * pair, pair)
        accq[rows, :] = lax.dot_general(
            wts[:, rows], dall[...], (((0,), (0,)), ((), ())), preferred_element_type=F32
        )
        if 2 * j >= nq // 2:
            for slot in (2 * j + 1, 2 * j):
                for p in range(PIECES):
                    rq(slot, p).start()

    def grad_d(j):
        rows = pl.ds(j * pair, pair)
        accd[rows, :] = jnp.dot(wts[rows, :], qall[...], preferred_element_type=F32)
        if 2 * j >= nd // 2:
            for slot in (2 * j + 1, 2 * j):
                for p in range(PIECES):
                    rd(slot, p).start()

    pairs_q, pairs_d = nq // 2, nd // 2
    for j in reversed(range(pairs_d // 2, pairs_d)):
        grad_d(j)
    for j in reversed(range(3 * pairs_q // 4, pairs_q)):
        grad_q(j)
    for j in reversed(range(pairs_q // 4, pairs_q // 2)):
        grad_q(j)
    for j in reversed(range(pairs_q // 2, 3 * pairs_q // 4)):
        grad_q(j)
    for j in reversed(range(pairs_q // 4)):
        grad_q(j)
    for j in reversed(range(pairs_d // 2)):
        grad_d(j)
    for copy in loss_copies:
        copy.start()

    def absorb(make, acc, got, slot, p):
        make(slot, p).wait_recv()
        into = slot - (1 << stage_of(slot))
        rows = pl.ds(into * c + p * piece, piece)
        acc[rows, :] = acc[rows, :] + got[pl.ds(slot * c + p * piece, piece), :]
        if into and stage_of(slot) == stage_of(into) + 1:
            make(into, p).start()

    def falling(high, low):
        return list(range(high - 1, low - 1, -1))

    order = [("q", t) for t in falling(nq, 3 * nq // 4)]
    order += [("d", t) for t in falling(nd, 3 * nd // 4)]
    order += [("q", t) for t in falling(3 * nq // 4, nq // 2)]
    rest_q, rest_d = falling(nq // 2, 1), falling(3 * nd // 4, 1)
    for i in range(max(len(rest_q), len(rest_d))):
        if i < len(rest_q):
            order.append(("q", rest_q[i]))
        if i < len(rest_d):
            order.append(("d", rest_d[i]))
    for which, slot in order:
        for p in range(PIECES):
            if which == "q":
                absorb(rq, accq, gotq, slot, p)
            else:
                absorb(rd, accd, gotd, slot, p)

    qn, qnorm = normalize(q_ref[...])
    outq_ref[...] = project(20.0 * accq[pl.ds(0, c), :], qn, qnorm)
    dn, dnorm = normalize(d_ref[...])
    outd_ref[...] = project(20.0 * accd[pl.ds(0, c), :], dn, dnorm)

    for copy in loss_copies:
        copy.wait_recv()
    row = tree_sum([losses[k] for k in range(nd)])
    loss_ref[...] = jnp.sum(row, axis=1, keepdims=True) / (c * n)

    for slot in range(1, nq):
        for p in range(PIECES):
            gq(slot, p).wait_send()
            rq(slot, p).wait_send()
    for slot in range(1, nd):
        for p in range(PIECES):
            gd(slot, p).wait_send()
            rd(slot, p).wait_send()
    for copy in pos_copies + stat_copies + loss_copies:
        copy.wait_send()


def local(queries, documents, positives):
    n = lax.axis_size("dp")
    c, width = queries.shape
    qbits, dbits = group_bits(n)
    nq, nd = 1 << len(qbits), 1 << len(dbits)
    dma = pltpu.SemaphoreType.DMA
    vmem = pl.BlockSpec(memory_space=pltpu.VMEM)
    loss, grad_q, grad_d = pl.pallas_call(
        functools.partial(kernel, n, qbits, dbits),
        out_shape=(
            jax.ShapeDtypeStruct((1, 1), F32),
            jax.ShapeDtypeStruct((c, width), F32),
            jax.ShapeDtypeStruct((c, width), F32),
        ),
        in_specs=[vmem] * 3,
        out_specs=(vmem, vmem, vmem),
        scratch_shapes=[
            pltpu.VMEM((nq * c, width), BF16),
            pltpu.VMEM((nd * c, width), BF16),
            pltpu.VMEM((1, nq * c), jnp.int32),
            pltpu.VMEM((nd * c, nq * c), F32),
            pltpu.VMEM((nd * c, nq * c), BF16),
            pltpu.VMEM((nq, 2, nq * c), F32),
            pltpu.VMEM((nd, 1, c), F32),
            pltpu.VMEM((nq * c, width), F32),
            pltpu.VMEM((nd * c, width), F32),
            pltpu.VMEM((nq * c, width), F32),
            pltpu.VMEM((nd * c, width), F32),
            dma((nq, PIECES)), dma((nq, PIECES)), dma((nd, PIECES)), dma((nd, PIECES)),
            dma((nq,)), dma((nq,)), dma((nq,)), dma((nq,)), dma((nd,)), dma((nd,)),
            dma((nq, PIECES)), dma((nq, PIECES)), dma((nd, PIECES)), dma((nd, PIECES)),
        ],
        compiler_params=pltpu.CompilerParams(
            collective_id=0, has_side_effects=True, vmem_limit_bytes=56 * 1024 * 1024
        ),
        cost_estimate=pl.CostEstimate(
            flops=6 * nq * c * nd * c * width,
            bytes_accessed=12 * c * width,
            transcendentals=nq * c * nd * c,
        ),
    )(queries, documents, positives.reshape(1, c))
    return (loss.reshape(()), grad_q, grad_d)


def solution(mesh):
    placed = (P("dp", None), P("dp", None), P("dp"))
    return jax.shard_map(
        local,
        mesh=mesh,
        in_specs=placed,
        out_specs=(P(), P("dp", None), P("dp", None)),
        check_vma=False,
    )
```

time: 276 us -> 62.8 us (0.23)
  waiting for transfers between devices: 167 us -> 0 us
  Pallas kernels: 0 us -> 57.7 us
  blocking collectives: 39.5 us -> 0 us
  matrix products: 31.9 us -> 0 us
  other arithmetic: 13.8 us -> 0 us
  between operations: 15.9 us -> 2.41 us
  local copies, waits for them, and re-layouts: 6.92 us -> 2.57 us
    reduce_scatter x1 -> x0, waiting for transfers between devices: 95.4 us -> none  [local(): lax.psum_scatter(20.0 * contract_rows(weights_of(rows, jnp.int32(0)), qb)...]
    all_gather x1 -> x0, waiting for transfers between devices: 71.2 us -> none  [local(): alldocs = lax.all_gather(db, 'dp', axis=0, tiled=True)]
    pallas_call x0 -> x1, Pallas kernels: none -> 57.7 us  [local(): pl.pallas_call(functools.partial(kernel, n, qbits, dbits), out_shape=(jax...]
    psum x1 -> x0, blocking collectives: 39.5 us -> none  [local(): loss_sum = lax.psum(jnp.sum(lse - positive_score), 'dp')]
    dot_general x9 -> x0, matrix products: 31.9 us -> none  [the longest x4 12.7 us: add_grad(): jnp.dot(weights, rows, preferred_element_type=jnp.float32)]
    reduce_sum x5 -> x0, other arithmetic: 4.66 us -> none  [the longest x2 2.09 us: normalize(): length = jnp.sqrt(jnp.sum(wide * wide, axis=1, keepdims=True) + 1e-06)]
    gather x1 -> x0, local copies, waits for them, and re-layouts: 4.56 us -> none  [local(): picked = jnp.take(alldocs, positives, axis=0)]
    add x9 -> x0, other arithmetic: 3.28 us -> none  [the longest x4 2.62 us: weights_of(): columns = start + lax.iota(jnp.int32, rows.shape[0])]
  transfers between devices with their start and end apart: 2 -> 0, of which waited for: 2 -> 0; matrix products, arithmetic and copies ran while one was open for 8% -> 0% of each run, Pallas kernels for 0% -> 0%
where the time goes in v1:
time: 62.8 us; the launch traced here: 62.7 us
  Pallas kernels  57.7 us (92%)
  local copies, waits for them, and re-layouts  2.57 us (4%)
  between operations  2.41 us (4%)
    pallas_call x1, Pallas kernels, local(): pl.pallas_call(functools.partial(kernel, n, qbits, dbits), out_shape=(jax...  57.7 us
    unnamed x4, local copies, waits for them, and re-layouts  2.57 us

profile of v1, /device:TPU:0, one launch (start us, length us, event | category | flops | bytes accessed | tf_op | source)
XLA Modules:
  0.0 62.7 jit_solution(2271758083934214733)
XLA Ops:
  0.6 57.7 %shard_map.58 = (f32[1,1]{1,0:T(1,128)}, f32[128,768]{1,0:T(8,128)}, f32[128,768]{1,0:T(8,128)}) custom-call(bf16[128,768]{1,0:T(8,128)(2,1)} %q_ref.1, bf16[128,768]{1,0:T(8,128)(2,1)} %d_ref.1, s32[1,128]{1,0:T(1,128)} %bitcast.2), custom_call_target="tpu_custom_call" | custom-call | flops 2415919104 | bytes 1179648 | tf_op jit(solution)/shard_map/pallas_call | solution.py:278
  58.9 0.0 copy-start
  59.0 1.8 %copy.10 = f32[128,768]{1,0:T(8,128)} copy(f32[128,768]{1,0:T(8,128)} %get-tuple-element.13) | data formatting | bytes 786432
  60.8 0.0 copy-done
  60.8 0.7 %copy.11 = f32[128,768]{1,0:T(8,128)} copy(f32[128,768]{1,0:T(8,128)S(1)} %copy-done) | data formatting | bytes 786432
Async XLA Ops:
  58.9 1.8 %copy-start = (f32[128,768]{1,0:T(8,128)S(1)}, f32[128,768]{1,0:T(8,128)}, u32[]{:S(2)}) copy-start(f32[128,768]{1,0:T(8,128)} %get-tuple-element.14) | copy-start | bytes 1179652

commit v2 on v1

v2 whole, which is shorter than its diff:
```python
import functools
import math

import jax
import jax.numpy as jnp
from jax import lax
from jax.experimental import pallas as pl
from jax.experimental.pallas import tpu as pltpu
from jax.sharding import PartitionSpec as P

PIECES = 2
F32 = jnp.float32
BF16 = jnp.bfloat16


def tree_sum(terms):
    while len(terms) > 1:
        terms = [terms[i] + terms[i + 1] for i in range(0, len(terms), 2)]
    return terms[0]


def normalize(values):
    wide = values.astype(F32)
    length = jnp.sqrt(jnp.sum(wide * wide, axis=1, keepdims=True) + 1e-06)
    return wide / length, length


def project(grad, unit, length):
    return (grad - jnp.sum(grad * unit, axis=1, keepdims=True) * unit) / length


def group_bits(n):
    bits = n.bit_length() - 1
    odd = [b for b in range(bits - 1, 0, -1) if b % 2 == 1]
    even = [b for b in range(bits - 1, 0, -1) if b % 2 == 0]
    return odd + [0], even


def stage_of(slot):
    return slot.bit_length() - 1


def place_of(slot, bits):
    return sum(((slot >> j) & 1) << (len(bits) - 1 - j) for j in range(len(bits)))


def falling(high, low):
    return list(range(high - 1, low - 1, -1))


def kernel(
    n, qbits, dbits,
    q_ref, d_ref, pos_ref,
    loss_ref, sumq_ref, sumd_ref,
    qall, dall, posrow, expd, wts, stats, losses, accq, accd, wideq,
    codeq, gotq, coded, gotd, scaleq, gotsq, scaled, gotsd,
    qs_sem, qr_sem, ds_sem, dr_sem, ps_sem, pr_sem, ss_sem, sr_sem, ls_sem, lr_sem,
    aqs_sem, aqr_sem, ads_sem, adr_sem, cqs_sem, cqr_sem, cds_sem, cdr_sem,
):
    me = lax.axis_index("dp")
    c, width = q_ref.shape
    piece = c // PIECES
    nq, nd = 1 << len(qbits), 1 << len(dbits)
    half = nq // 2

    def flipped(bits, slot):
        where = me
        for j, b in enumerate(bits):
            if (slot >> j) & 1:
                where = where + (1 - 2 * (lax.rem(lax.div(me, 1 << b), 2))) * (1 << b)
        return where

    def place_q(slot):
        return place_of(slot, qbits)

    def place_d(slot):
        return place_of(slot, dbits)

    peer_q = [flipped(qbits, k) for k in range(nq)]
    peer_d = [flipped(dbits, k) for k in range(nd)]

    barrier = pltpu.get_barrier_semaphore()
    for peer in peer_q[1:] + peer_d[1:]:
        pl.semaphore_signal(barrier, inc=1, device_id=(peer,), device_id_type=pl.DeviceIdType.MESH)

    qall[pl.ds(0, c), :] = normalize(q_ref[...])[0].astype(BF16)
    dall[pl.ds(0, c), :] = normalize(d_ref[...])[0].astype(BF16)
    posrow[:, pl.ds(0, c)] = pos_ref[...]

    pl.semaphore_wait(barrier, nq + nd - 2)

    def remote(src, dst, send, recv, peer):
        return pltpu.make_async_remote_copy(
            src_ref=src, dst_ref=dst, send_sem=send, recv_sem=recv,
            device_id=(peer,), device_id_type=pl.DeviceIdType.MESH,
        )

    def gather_copy(buf, place, send, recv, peers, slot, p):
        low = slot - (1 << stage_of(slot))
        return remote(
            buf.at[pl.ds(place(low) * c + p * piece, piece), :],
            buf.at[pl.ds(place(slot) * c + p * piece, piece), :],
            send.at[slot, p], recv.at[slot, p], peers[1 << stage_of(slot)],
        )

    gq = functools.partial(gather_copy, qall, place_q, qs_sem, qr_sem, peer_q)
    gd = functools.partial(gather_copy, dall, place_d, ds_sem, dr_sem, peer_d)
    pos_copies = [
        remote(posrow.at[:, pl.ds(0, c)], posrow.at[:, pl.ds(place_q(k) * c, c)],
               ps_sem.at[k], pr_sem.at[k], peer_q[k])
        for k in range(1, nq)
    ]

    for make, bits in ((gq, qbits), (gd, dbits)):
        for p in range(PIECES):
            for j in range(len(bits)):
                make(1 << j, p).start()
    for copy in pos_copies:
        copy.start()

    def arrive(make, bits, slots):
        for slot in slots:
            for p in range(PIECES):
                make(slot, p).wait_recv()
                for j in range(stage_of(slot) + 1, len(bits)):
                    make(slot + (1 << j), p).start()

    pair = 2 * c
    bases = [peer_d[place_d(i)] * c for i in range(nd)]

    def hits(j, i):
        start = j * pair if isinstance(j, int) else pl.multiple_of(j * pair, pair)
        return lax.broadcasted_iota(jnp.int32, (c, pair), 0) == posrow[:, pl.ds(start, pair)] - bases[i]

    def score(pairs, upper):
        first = nd // 2 if upper else 0

        def step(j, carry):
            lanes = pl.ds(pl.multiple_of(j * pair, pair), pair)
            if upper:
                total, picked = stats[0, 0:1, lanes], stats[0, 1:2, lanes]
            else:
                total, picked = jnp.zeros((1, pair), F32), jnp.zeros((1, pair), F32)
            dots = lax.dot_general(
                dall[pl.ds(first * c, nd // 2 * c), :], qall[lanes, :],
                (((1,), (1,)), ((), ())), preferred_element_type=F32,
            )
            for i in range(nd // 2):
                scores = 20.0 * dots[i * c:(i + 1) * c, :]
                powers = jnp.exp(scores - 20.0)
                expd[pl.ds((first + i) * c, c), lanes] = powers
                total = total + jnp.sum(powers, axis=0, keepdims=True)
                picked = picked + jnp.sum(
                    jnp.where(hits(j, first + i), scores, 0.0), axis=0, keepdims=True
                )
            stats[0, 0:1, lanes] = total
            stats[0, 1:2, lanes] = picked
            return carry

        lax.fori_loop(pairs[0], pairs[1], step, 0)

    arrive(gq, qbits, [1])
    arrive(gq, qbits, range(2, nq, 2))
    arrive(gd, dbits, range(2, nd, 2))
    for copy in pos_copies:
        copy.wait_recv()
    score((0, nq // 4), False)
    arrive(gd, dbits, [1])
    arrive(gq, qbits, [3])
    arrive(gq, qbits, range(5, nq, 4))
    score((nq // 4, 3 * nq // 8), False)
    arrive(gd, dbits, range(3, nd, 2))
    score((0, 3 * nq // 8), True)
    arrive(gq, qbits, range(7, nq, 4))
    score((3 * nq // 8, nq // 2), False)
    score((3 * nq // 8, nq // 2), True)

    stat_copies = [
        remote(stats.at[0], stats.at[k], ss_sem.at[k], sr_sem.at[k], peer_q[k])
        for k in range(1, nq)
    ]
    for copy in stat_copies:
        copy.start()
    for copy in stat_copies:
        copy.wait_recv()

    def slot_total(row, r):
        return tree_sum(
            [stats[k, row:row + 1, pl.ds(place_q(r ^ k) * c, c)] for k in range(nq)]
        )

    totals = [slot_total(0, r) for r in range(nq)]
    losses[0] = tree_sum([20.0 + jnp.log(totals[r]) - slot_total(1, r) for r in range(nq)])
    loss_copies = [
        remote(losses.at[0], losses.at[k], ls_sem.at[k], lr_sem.at[k], peer_d[k])
        for k in range(1, nd)
    ]

    for j in range(nq // 2):
        inverse = 1.0 / jnp.concatenate(
            [totals[place_q(2 * j)], totals[place_q(2 * j + 1)]], axis=1
        )
        lanes = pl.ds(j * pair, pair)
        for i in range(nd):
            rows = pl.ds(i * c, c)
            hit = jnp.where(hits(j, i), 1.0, 0.0)
            wts[rows, lanes] = (expd[rows, lanes] * inverse - hit).astype(BF16)

    diagonal = lax.broadcasted_iota(jnp.int32, (piece, 128), 0) == lax.broadcasted_iota(
        jnp.int32, (piece, 128), 1
    )

    def narrow_copies(code, got, scale, gots, sems, peers, slot, p):
        rows = pl.ds(slot * c + p * piece, piece)
        line = slot * PIECES + p
        peer = peers[1 << stage_of(slot)]
        return (
            remote(code.at[rows, :], got.at[rows, :], sems[0].at[slot, p], sems[1].at[slot, p], peer),
            remote(scale.at[line], gots.at[line], sems[2].at[slot, p], sems[3].at[slot, p], peer),
        )

    nq_copies = functools.partial(
        narrow_copies, codeq, gotq, scaleq, gotsq, (aqs_sem, aqr_sem, cqs_sem, cqr_sem), peer_q
    )
    nd_copies = functools.partial(
        narrow_copies, coded, gotd, scaled, gotsd, (ads_sem, adr_sem, cds_sem, cdr_sem), peer_d
    )

    def wide_copy(slot, p):
        return remote(
            accq.at[pl.ds(place_q(slot) * c + p * piece, piece), :],
            wideq.at[pl.ds((slot - half) * c + p * piece, piece), :],
            aqs_sem.at[slot, p], aqr_sem.at[slot, p], peer_q[half],
        )

    def send(which, slot, p):
        if which == "q" and slot >= half:
            wide_copy(slot, p).start()
            return
        acc, place, code, scale, copies = (
            (accq, place_q, codeq, scaleq, nq_copies) if which == "q"
            else (accd, place_d, coded, scaled, nd_copies)
        )
        value = acc[pl.ds(place(slot) * c + p * piece, piece), :]
        top = jnp.maximum(jnp.max(jnp.abs(value), axis=1, keepdims=True), 1e-30)
        codes = jnp.round(value * (32767.0 / top))
        code[pl.ds(slot * c + p * piece, piece), :] = codes.astype(jnp.int32).astype(jnp.int16)
        scale[slot * PIECES + p] = jnp.sum(
            jnp.where(diagonal, top * (1.0 / 32767.0), 0.0), axis=0, keepdims=True
        )
        for copy in copies(slot, p):
            copy.start()

    def absorb(which, slots):
        for slot in slots:
            into = slot - (1 << stage_of(slot))
            for p in range(PIECES):
                if which == "q" and slot >= half:
                    wide_copy(slot, p).wait_recv()
                    value = wideq[pl.ds((slot - half) * c + p * piece, piece), :]
                else:
                    got, gots, copies = (
                        (gotq, gotsq, nq_copies) if which == "q" else (gotd, gotsd, nd_copies)
                    )
                    for copy in copies(slot, p):
                        copy.wait_recv()
                    scales = jnp.sum(
                        jnp.where(diagonal, gots[slot * PIECES + p], 0.0), axis=1, keepdims=True
                    )
                    codes = got[pl.ds(slot * c + p * piece, piece), :]
                    value = codes.astype(jnp.int32).astype(F32) * scales
                acc, place = (accq, place_q) if which == "q" else (accd, place_d)
                rows = pl.ds(place(into) * c + p * piece, piece)
                acc[rows, :] = acc[rows, :] + value
                if into and stage_of(slot) == stage_of(into) + 1:
                    send(which, into, p)

    def grad_q(slots):
        for slot in slots:
            rows = pl.ds(place_q(slot) * c, pair)
            accq[rows, :] = lax.dot_general(
                wts[:, rows], dall[...], (((0,), (0,)), ((), ())), preferred_element_type=F32
            )
            for p in range(PIECES):
                send("q", slot + half, p)

    def grad_d(slots):
        for slot in slots:
            rows = pl.ds(place_d(slot) * c, pair)
            accd[rows, :] = jnp.dot(wts[rows, :], qall[...], preferred_element_type=F32)
            for p in range(PIECES):
                send("d", slot + nd // 2, p)

    early_q, late_q = falling(half, half // 2), falling(half // 2, 0)
    grad_q(early_q[:1])
    grad_d(falling(nd // 2, nd // 4))
    grad_q(early_q[1:])
    absorb("q", [early_q[0] + half])
    grad_d(falling(nd // 4, 0))
    absorb("q", [slot + half for slot in early_q[1:]])
    grad_q(late_q)
    for copy in loss_copies:
        copy.start()

    absorb("d", falling(nd, 3 * nd // 4))
    absorb("q", [slot + half for slot in late_q])
    rest_q, rest_d = falling(half, 1), falling(3 * nd // 4, 1)
    for i in range(max(len(rest_q), len(rest_d))):
        absorb("q", rest_q[i:i + 1])
        absorb("d", rest_d[i:i + 1])

    sumq_ref[...] = 20.0 * accq[pl.ds(0, c), :]
    sumd_ref[...] = 20.0 * accd[pl.ds(0, c), :]

    for copy in loss_copies:
        copy.wait_recv()
    row = tree_sum([losses[k] for k in range(nd)])
    loss_ref[...] = jnp.sum(row, axis=1, keepdims=True) / (c * n)

    for p in range(PIECES):
        for slot in range(1, nq):
            gq(slot, p).wait_send()
            for copy in nq_copies(slot, p) if slot < half else (wide_copy(slot, p),):
                copy.wait_send()
        for slot in range(1, nd):
            gd(slot, p).wait_send()
            for copy in nd_copies(slot, p):
                copy.wait_send()
    for copy in pos_copies + stat_copies + loss_copies:
        copy.wait_send()


def finish(q_ref, d_ref, sumq_ref, sumd_ref, outq_ref, outd_ref):
    outq_ref[...] = project(sumq_ref[...], *normalize(q_ref[...]))
    outd_ref[...] = project(sumd_ref[...], *normalize(d_ref[...]))


def local(queries, documents, positives):
    n = lax.axis_size("dp")
    c, width = queries.shape
    qbits, dbits = group_bits(n)
    nq, nd = 1 << len(qbits), 1 << len(dbits)
    dma = pltpu.SemaphoreType.DMA
    vmem = pl.BlockSpec(memory_space=pltpu.VMEM)
    tile = jax.ShapeDtypeStruct((c, width), F32)
    buffers = [
        ((nq * c, width), BF16),
        ((nd * c, width), BF16),
        ((1, nq * c), jnp.int32),
        ((nd * c, nq * c), F32),
        ((nd * c, nq * c), BF16),
        ((nq, 2, nq * c), F32),
        ((nd, 1, c), F32),
        ((nq * c, width), F32),
        ((nd * c, width), F32),
        ((nq // 2 * c, width), F32),
        ((nq // 2 * c, width), jnp.int16),
        ((nq // 2 * c, width), jnp.int16),
        ((nd * c, width), jnp.int16),
        ((nd * c, width), jnp.int16),
        ((nq // 2 * PIECES, 1, 128), F32),
        ((nq // 2 * PIECES, 1, 128), F32),
        ((nd * PIECES, 1, 128), F32),
        ((nd * PIECES, 1, 128), F32),
    ]
    held = sum(math.prod(shape) * jnp.dtype(kind).itemsize for shape, kind in buffers)
    loss, sum_q, sum_d = pl.pallas_call(
        functools.partial(kernel, n, qbits, dbits),
        out_shape=(jax.ShapeDtypeStruct((1, 1), F32), tile, tile),
        in_specs=[vmem] * 3,
        out_specs=(vmem, vmem, vmem),
        scratch_shapes=[pltpu.VMEM(shape, kind) for shape, kind in buffers] + [
            dma((nq, PIECES)), dma((nq, PIECES)), dma((nd, PIECES)), dma((nd, PIECES)),
            dma((nq,)), dma((nq,)), dma((nq,)), dma((nq,)), dma((nd,)), dma((nd,)),
            dma((nq, PIECES)), dma((nq, PIECES)), dma((nd, PIECES)), dma((nd, PIECES)),
            dma((nq, PIECES)), dma((nq, PIECES)), dma((nd, PIECES)), dma((nd, PIECES)),
        ],
        compiler_params=pltpu.CompilerParams(
            collective_id=0, has_side_effects=True,
            vmem_limit_bytes=min(held + (12 << 20), 56 << 20),
        ),
        cost_estimate=pl.CostEstimate(
            flops=6 * nq * c * nd * c * width,
            bytes_accessed=12 * c * width,
            transcendentals=nq * c * nd * c,
        ),
    )(queries, documents, positives.reshape(1, c))
    grad_q, grad_d = pl.pallas_call(
        finish,
        out_shape=(tile, tile),
        in_specs=[vmem] * 4,
        out_specs=(vmem, vmem),
        cost_estimate=pl.CostEstimate(
            flops=16 * c * width, bytes_accessed=20 * c * width, transcendentals=0
        ),
    )(queries, documents, sum_q, sum_d)
    return (loss.reshape(()), grad_q, grad_d)


def solution(mesh):
    placed = (P("dp", None), P("dp", None), P("dp"))
    return jax.shard_map(
        local,
        mesh=mesh,
        in_specs=placed,
        out_specs=(P(), P("dp", None), P("dp", None)),
        check_vma=False,
    )
```

time: 62.8 us -> 57.8 us (0.920)
  Pallas kernels: 57.7 us -> 51.2 us
  local copies, waits for them, and re-layouts: 2.57 us -> 4.01 us
    pallas_call x1, Pallas kernels: 57.7 us -> 48.7 us  [local(): pl.pallas_call(functools.partial(kernel, n, qbits, dbits), out_shape=(jax...]
    pallas_call x0 -> x1, Pallas kernels: none -> 2.46 us  [local(): pl.pallas_call(finish, out_shape=(tile, tile), in_specs=[vmem] * 4, out_s...]
    unnamed x4 -> x10, local copies, waits for them, and re-layouts: 2.57 us -> 4.01 us
where the time goes in v2:
time: 57.8 us; the launch traced here: 57.6 us
  Pallas kernels  51.2 us (89%)
  local copies, waits for them, and re-layouts  4.01 us (7%)
  between operations  2.46 us (4%)
    pallas_call x1, Pallas kernels, local(): pl.pallas_call(functools.partial(kernel, n, qbits, dbits), out_shape=(jax...  48.7 us
    unnamed x10, local copies, waits for them, and re-layouts  4.01 us
    pallas_call x1, Pallas kernels, local(): pl.pallas_call(finish, out_shape=(tile, tile), in_specs=[vmem] * 4, out_s...  2.46 us

profile of v2, /device:TPU:0, one launch (start us, length us, event | category | flops | bytes accessed | tf_op | source)
XLA Modules:
  0.0 57.6 jit_solution(13038158464851375845)
XLA Ops:
  0.6 0.0 copy-start.4
  0.6 0.6 %copy-done.4 = s32[128]{0:T(128)S(1)} copy-done((s32[128]{0:T(128)S(1)}, s32[128]{0:T(128)}, u32[]{:S(2)}) %copy-start.4) | copy-done | bytes 536
  1.3 0.0 copy-start.2
  1.3 0.9 %copy-done.2 = bf16[128,768]{1,0:T(8,128)(2,1)S(1)} copy-done((bf16[128,768]{1,0:T(8,128)(2,1)S(1)}, bf16[128,768]{1,0:T(8,128)(2,1)}, u32[]{:S(2)}) %copy-start.2) | copy-done | bytes 196632
  2.2 0.0 copy-start.3
  2.2 0.9 %copy-done.3 = bf16[128,768]{1,0:T(8,128)(2,1)S(1)} copy-done((bf16[128,768]{1,0:T(8,128)(2,1)S(1)}, bf16[128,768]{1,0:T(8,128)(2,1)}, u32[]{:S(2)}) %copy-start.3) | copy-done | bytes 196632
  3.1 48.7 %shard_map.58 = (f32[1,1]{1,0:T(1,128)}, f32[128,768]{1,0:T(8,128)S(1)}, f32[128,768]{1,0:T(8,128)S(1)}) custom-call(bf16[128,768]{1,0:T(8,128)(2,1)S(1)} %copy-done.2, bf16[128,768]{1,0:T(8,128)(2,1)S(1)} %copy-done.3, s32[1,128]{1,0:T(1,128)S(1)} %bitcast.2), custom_call_target="tpu_custom_call" | custom-call | flops 2415919104 | bytes 1179648 | tf_op jit(solution)/shard_map/pallas_call | solution.py:367
  51.8 0.0 copy-start
  51.9 0.7 %copy-done = f32[128,768]{1,0:T(8,128)} copy-done((f32[128,768]{1,0:T(8,128)}, f32[128,768]{1,0:T(8,128)S(1)}, u32[]{:S(2)}) %copy-start) | copy-done | bytes 393240
  52.6 0.0 copy-start.1
  52.6 0.8 %copy-done.1 = f32[128,768]{1,0:T(8,128)} copy-done((f32[128,768]{1,0:T(8,128)}, f32[128,768]{1,0:T(8,128)S(1)}, u32[]{:S(2)}) %copy-start.1) | copy-done | bytes 393240
  53.4 2.5 %shard_map.59 = (f32[128,768]{1,0:T(8,128)}, f32[128,768]{1,0:T(8,128)}) custom-call(bf16[128,768]{1,0:T(8,128)(2,1)} %q_ref.3, bf16[128,768]{1,0:T(8,128)(2,1)} %d_ref.3, f32[128,768]{1,0:T(8,128)} %copy-done, f32[128,768]{1,0:T(8,128)} %copy-done.1), custom_call_target="tpu_custom_call" | custom-call | flops 1572864 | bytes 1966080 | tf_op jit(solution)/shard_map/pallas_call | solution.py:388
Async XLA Ops:
  0.6 0.7 %copy-start.4 = (s32[128]{0:T(128)S(1)}, s32[128]{0:T(128)}, u32[]{:S(2)}) copy-start(s32[128]{0:T(128)} %param.5) | copy-start | bytes 1540
  1.3 0.9 %copy-start.2 = (bf16[128,768]{1,0:T(8,128)(2,1)S(1)}, bf16[128,768]{1,0:T(8,128)(2,1)}, u32[]{:S(2)}) copy-start(bf16[128,768]{1,0:T(8,128)(2,1)} %q_ref.3) | copy-start | bytes 589828
  2.2 0.9 %copy-start.3 = (bf16[128,768]{1,0:T(8,128)(2,1)S(1)}, bf16[128,768]{1,0:T(8,128)(2,1)}, u32[]{:S(2)}) copy-start(bf16[128,768]{1,0:T(8,128)(2,1)} %d_ref.3) | copy-start | bytes 589828
  51.8 0.8 %copy-start = (f32[128,768]{1,0:T(8,128)}, f32[128,768]{1,0:T(8,128)S(1)}, u32[]{:S(2)}) copy-start(f32[128,768]{1,0:T(8,128)S(1)} %get-tuple-element.9.sumq_ref) | copy-start | bytes 1179652
  52.6 0.8 %copy-start.1 = (f32[128,768]{1,0:T(8,128)}, f32[128,768]{1,0:T(8,128)S(1)}, u32[]{:S(2)}) copy-start(f32[128,768]{1,0:T(8,128)S(1)} %get-tuple-element.10.sumd_ref) | copy-start | bytes 1179652

commit v3 on v2

--- a/solution.py
+++ b/solution.py
@@ -1,5 +1,4 @@
 import functools
-import math
 
 import jax
 import jax.numpy as jnp
@@ -51,11 +50,11 @@
 def kernel(
     n, qbits, dbits,
     q_ref, d_ref, pos_ref,
-    loss_ref, sumq_ref, sumd_ref,
-    qall, dall, posrow, expd, wts, stats, losses, accq, accd, wideq,
+    loss_ref, outq_ref, outd_ref,
+    qown, down, qall, dall, posrow, expd, wts, stats, losses, accq, accd, wideq,
     codeq, gotq, coded, gotd, scaleq, gotsq, scaled, gotsd,
     qs_sem, qr_sem, ds_sem, dr_sem, ps_sem, pr_sem, ss_sem, sr_sem, ls_sem, lr_sem,
-    aqs_sem, aqr_sem, ads_sem, adr_sem, cqs_sem, cqr_sem, cds_sem, cdr_sem,
+    aqs_sem, aqr_sem, ads_sem, adr_sem, cqs_sem, cqr_sem, cds_sem, cdr_sem, io_sem,
 ):
     me = lax.axis_index("dp")
     c, width = q_ref.shape
@@ -79,13 +78,21 @@
     peer_q = [flipped(qbits, k) for k in range(nq)]
     peer_d = [flipped(dbits, k) for k in range(nd)]
 
+    loads = [
+        pltpu.make_async_copy(q_ref, qown, io_sem.at[0]),
+        pltpu.make_async_copy(d_ref, down, io_sem.at[1]),
+        pltpu.make_async_copy(pos_ref, posrow.at[:, pl.ds(0, c)], io_sem.at[2]),
+    ]
+    for copy in loads:
+        copy.start()
     barrier = pltpu.get_barrier_semaphore()
     for peer in peer_q[1:] + peer_d[1:]:
         pl.semaphore_signal(barrier, inc=1, device_id=(peer,), device_id_type=pl.DeviceIdType.MESH)
 
-    qall[pl.ds(0, c), :] = normalize(q_ref[...])[0].astype(BF16)
-    dall[pl.ds(0, c), :] = normalize(d_ref[...])[0].astype(BF16)
-    posrow[:, pl.ds(0, c)] = pos_ref[...]
+    for copy in loads:
+        copy.wait()
+    qall[pl.ds(0, c), :] = normalize(qown[...])[0].astype(BF16)
+    dall[pl.ds(0, c), :] = normalize(down[...])[0].astype(BF16)
 
     pl.semaphore_wait(barrier, nq + nd - 2)
 
@@ -132,26 +139,25 @@
         start = j * pair if isinstance(j, int) else pl.multiple_of(j * pair, pair)
         return lax.broadcasted_iota(jnp.int32, (c, pair), 0) == posrow[:, pl.ds(start, pair)] - bases[i]
 
-    def score(pairs, upper):
-        first = nd // 2 if upper else 0
+    def score(pairs, first, last):
 
         def step(j, carry):
             lanes = pl.ds(pl.multiple_of(j * pair, pair), pair)
-            if upper:
+            if first:
                 total, picked = stats[0, 0:1, lanes], stats[0, 1:2, lanes]
             else:
                 total, picked = jnp.zeros((1, pair), F32), jnp.zeros((1, pair), F32)
             dots = lax.dot_general(
-                dall[pl.ds(first * c, nd // 2 * c), :], qall[lanes, :],
+                dall[pl.ds(first * c, (last - first) * c), :], qall[lanes, :],
                 (((1,), (1,)), ((), ())), preferred_element_type=F32,
             )
-            for i in range(nd // 2):
-                scores = 20.0 * dots[i * c:(i + 1) * c, :]
+            for i in range(first, last):
+                scores = 20.0 * dots[(i - first) * c:(i - first + 1) * c, :]
                 powers = jnp.exp(scores - 20.0)
-                expd[pl.ds((first + i) * c, c), lanes] = powers
+                expd[pl.ds(i * c, c), lanes] = powers
                 total = total + jnp.sum(powers, axis=0, keepdims=True)
                 picked = picked + jnp.sum(
-                    jnp.where(hits(j, first + i), scores, 0.0), axis=0, keepdims=True
+                    jnp.where(hits(j, i), scores, 0.0), axis=0, keepdims=True
                 )
             stats[0, 0:1, lanes] = total
             stats[0, 1:2, lanes] = picked
@@ -164,16 +170,18 @@
     arrive(gd, dbits, range(2, nd, 2))
     for copy in pos_copies:
         copy.wait_recv()
-    score((0, nq // 4), False)
+    low, high = nd // 2, 3 * nd // 4
+    score((0, nq // 4), 0, low)
     arrive(gd, dbits, [1])
     arrive(gq, qbits, [3])
     arrive(gq, qbits, range(5, nq, 4))
-    score((nq // 4, 3 * nq // 8), False)
-    arrive(gd, dbits, range(3, nd, 2))
-    score((0, 3 * nq // 8), True)
+    arrive(gd, dbits, range(5, nd, 4))
+    score((nq // 4, 3 * nq // 8), 0, low)
+    score((0, 3 * nq // 8), low, high)
     arrive(gq, qbits, range(7, nq, 4))
-    score((3 * nq // 8, nq // 2), False)
-    score((3 * nq // 8, nq // 2), True)
+    score((3 * nq // 8, nq // 2), 0, high)
+    arrive(gd, dbits, range(3, nd, 4))
+    score((0, nq // 2), high, nd)
 
     stat_copies = [
         remote(stats.at[0], stats.at[k], ss_sem.at[k], sr_sem.at[k], peer_q[k])
@@ -292,9 +300,8 @@
                 send("d", slot + nd // 2, p)
 
     early_q, late_q = falling(half, half // 2), falling(half // 2, 0)
-    grad_q(early_q[:1])
     grad_d(falling(nd // 2, nd // 4))
-    grad_q(early_q[1:])
+    grad_q(early_q)
     absorb("q", [early_q[0] + half])
     grad_d(falling(nd // 4, 0))
     absorb("q", [slot + half for slot in early_q[1:]])
@@ -309,8 +316,15 @@
         absorb("q", rest_q[i:i + 1])
         absorb("d", rest_d[i:i + 1])
 
-    sumq_ref[...] = 20.0 * accq[pl.ds(0, c), :]
-    sumd_ref[...] = 20.0 * accd[pl.ds(0, c), :]
+    own = pl.ds(0, c)
+    stores = [
+        pltpu.make_async_copy(accq.at[own, :], outq_ref, io_sem.at[3]),
+        pltpu.make_async_copy(accd.at[own, :], outd_ref, io_sem.at[4]),
+    ]
+    accq[own, :] = project(20.0 * accq[own, :], *normalize(qown[...]))
+    stores[0].start()
+    accd[own, :] = project(20.0 * accd[own, :], *normalize(down[...]))
+    stores[1].start()
 
     for copy in loss_copies:
         copy.wait_recv()
@@ -328,11 +342,8 @@
                 copy.wait_send()
     for copy in pos_copies + stat_copies + loss_copies:
         copy.wait_send()
-
-
-def finish(q_ref, d_ref, sumq_ref, sumd_ref, outq_ref, outd_ref):
-    outq_ref[...] = project(sumq_ref[...], *normalize(q_ref[...]))
-    outd_ref[...] = project(sumd_ref[...], *normalize(d_ref[...]))
+    for copy in stores:
+        copy.wait()
 
 
 def local(queries, documents, positives):
@@ -343,7 +354,10 @@
     dma = pltpu.SemaphoreType.DMA
     vmem = pl.BlockSpec(memory_space=pltpu.VMEM)
     tile = jax.ShapeDtypeStruct((c, width), F32)
+    anywhere = pl.BlockSpec(memory_space=pl.ANY)
     buffers = [
+        ((c, width), BF16),
+        ((c, width), BF16),
         ((nq * c, width), BF16),
         ((nd * c, width), BF16),
         ((1, nq * c), jnp.int32),
@@ -363,21 +377,21 @@
         ((nd * PIECES, 1, 128), F32),
         ((nd * PIECES, 1, 128), F32),
     ]
-    held = sum(math.prod(shape) * jnp.dtype(kind).itemsize for shape, kind in buffers)
-    loss, sum_q, sum_d = pl.pallas_call(
+    loss, grad_q, grad_d = pl.pallas_call(
         functools.partial(kernel, n, qbits, dbits),
         out_shape=(jax.ShapeDtypeStruct((1, 1), F32), tile, tile),
-        in_specs=[vmem] * 3,
-        out_specs=(vmem, vmem, vmem),
+        in_specs=[anywhere] * 3,
+        out_specs=(vmem, anywhere, anywhere),
         scratch_shapes=[pltpu.VMEM(shape, kind) for shape, kind in buffers] + [
             dma((nq, PIECES)), dma((nq, PIECES)), dma((nd, PIECES)), dma((nd, PIECES)),
             dma((nq,)), dma((nq,)), dma((nq,)), dma((nq,)), dma((nd,)), dma((nd,)),
             dma((nq, PIECES)), dma((nq, PIECES)), dma((nd, PIECES)), dma((nd, PIECES)),
             dma((nq, PIECES)), dma((nq, PIECES)), dma((nd, PIECES)), dma((nd, PIECES)),
+            dma((5,)),
         ],
         compiler_params=pltpu.CompilerParams(
             collective_id=0, has_side_effects=True,
-            vmem_limit_bytes=min(held + (12 << 20), 56 << 20),
+            vmem_limit_bytes=56 << 20,
         ),
         cost_estimate=pl.CostEstimate(
             flops=6 * nq * c * nd * c * width,
@@ -385,15 +399,6 @@
             transcendentals=nq * c * nd * c,
         ),
     )(queries, documents, positives.reshape(1, c))
-    grad_q, grad_d = pl.pallas_call(
-        finish,
-        out_shape=(tile, tile),
-        in_specs=[vmem] * 4,
-        out_specs=(vmem, vmem),
-        cost_estimate=pl.CostEstimate(
-            flops=16 * c * width, bytes_accessed=20 * c * width, transcendentals=0
-        ),
-    )(queries, documents, sum_q, sum_d)
     return (loss.reshape(()), grad_q, grad_d)
 
 

time: 57.8 us -> 54.9 us (0.950)
  Pallas kernels: 51.2 us -> 49.7 us
  local copies, waits for them, and re-layouts: 4.01 us -> 2.57 us
    pallas_call x1 -> x0, Pallas kernels: 2.46 us -> none  [local(): pl.pallas_call(finish, out_shape=(tile, tile), in_specs=[vmem] * 4, out_s...]
    unnamed x10 -> x4, local copies, waits for them, and re-layouts: 4.01 us -> 2.57 us
    pallas_call x1, Pallas kernels: 48.7 us -> 49.7 us  [local(): pl.pallas_call(functools.partial(kernel, n, qbits, dbits), out_shape=(jax...]
where the time goes in v3:
time: 54.9 us; the launch traced here: 54.7 us
  Pallas kernels  49.7 us (91%)
  local copies, waits for them, and re-layouts  2.57 us (5%)
  between operations  2.41 us (4%)
    pallas_call x1, Pallas kernels, local(): pl.pallas_call(functools.partial(kernel, n, qbits, dbits), out_shape=(jax...  49.7 us
    unnamed x4, local copies, waits for them, and re-layouts  2.57 us

profile of v3, /device:TPU:0, one launch (start us, length us, event | category | flops | bytes accessed | tf_op | source)
XLA Modules:
  0.0 54.7 jit_solution(4269391347290366616)
XLA Ops:
  0.6 49.7 %shard_map.58 = (f32[1,1]{1,0:T(1,128)}, f32[128,768]{1,0:T(8,128)}, f32[128,768]{1,0:T(8,128)}) custom-call(bf16[128,768]{1,0:T(8,128)(2,1)} %q_ref.1, bf16[128,768]{1,0:T(8,128)(2,1)} %d_ref.1, s32[1,128]{1,0:T(1,128)} %bitcast.2), custom_call_target="tpu_custom_call" | custom-call | flops 2415919104 | bytes 1179648 | tf_op jit(solution)/shard_map/pallas_call | solution.py:380
  51.0 0.0 copy-start
  51.0 1.8 %copy.10 = f32[128,768]{1,0:T(8,128)} copy(f32[128,768]{1,0:T(8,128)} %get-tuple-element.13) | data formatting | bytes 786432
  52.8 0.0 copy-done
  52.8 0.7 %copy.11 = f32[128,768]{1,0:T(8,128)} copy(f32[128,768]{1,0:T(8,128)S(1)} %copy-done) | data formatting | bytes 786432
Async XLA Ops:
  51.0 1.8 %copy-start = (f32[128,768]{1,0:T(8,128)S(1)}, f32[128,768]{1,0:T(8,128)}, u32[]{:S(2)}) copy-start(f32[128,768]{1,0:T(8,128)} %get-tuple-element.14) | copy-start | bytes 1179652

commit v4 on v3

--- a/solution.py
+++ b/solution.py
@@ -8,6 +8,7 @@
 from jax.sharding import PartitionSpec as P
 
 PIECES = 2
+VMEM_BYTES = 56 << 20
 F32 = jnp.float32
 BF16 = jnp.bfloat16
 
@@ -118,10 +119,11 @@
         for k in range(1, nq)
     ]
 
-    for make, bits in ((gq, qbits), (gd, dbits)):
-        for p in range(PIECES):
-            for j in range(len(bits)):
-                make(1 << j, p).start()
+    for p in range(PIECES):
+        for j in range(len(qbits)):
+            gq(1 << j, p).start()
+            if j < len(dbits):
+                gd(1 << j, p).start()
     for copy in pos_copies:
         copy.start()
 
@@ -163,7 +165,7 @@
             stats[0, 1:2, lanes] = picked
             return carry
 
-        lax.fori_loop(pairs[0], pairs[1], step, 0)
+        lax.fori_loop(pairs[0], pairs[1], step, 0, unroll=True)
 
     arrive(gq, qbits, [1])
     arrive(gq, qbits, range(2, nq, 2))
@@ -204,15 +206,18 @@
         for k in range(1, nd)
     ]
 
-    for j in range(nq // 2):
-        inverse = 1.0 / jnp.concatenate(
-            [totals[place_q(2 * j)], totals[place_q(2 * j + 1)]], axis=1
-        )
-        lanes = pl.ds(j * pair, pair)
-        for i in range(nd):
+    inverses = [
+        1.0 / jnp.concatenate([totals[place_q(2 * j)], totals[place_q(2 * j + 1)]], axis=1)
+        for j in range(nq // 2)
+    ]
+
+    def weigh(places):
+        for i in places:
             rows = pl.ds(i * c, c)
-            hit = jnp.where(hits(j, i), 1.0, 0.0)
-            wts[rows, lanes] = (expd[rows, lanes] * inverse - hit).astype(BF16)
+            for j in range(nq // 2):
+                lanes = pl.ds(j * pair, pair)
+                hit = jnp.where(hits(j, i), 1.0, 0.0)
+                wts[rows, lanes] = (expd[rows, lanes] * inverses[j] - hit).astype(BF16)
 
     diagonal = lax.broadcasted_iota(jnp.int32, (piece, 128), 0) == lax.broadcasted_iota(
         jnp.int32, (piece, 128), 1
@@ -300,7 +305,11 @@
                 send("d", slot + nd // 2, p)
 
     early_q, late_q = falling(half, half // 2), falling(half // 2, 0)
-    grad_d(falling(nd // 2, nd // 4))
+    for slot in falling(nd // 2, nd // 4):
+        weigh([place_d(slot), place_d(slot) + 1])
+        grad_d([slot])
+    for slot in falling(nd // 4, 0):
+        weigh([place_d(slot), place_d(slot) + 1])
     grad_q(early_q)
     absorb("q", [early_q[0] + half])
     grad_d(falling(nd // 4, 0))
@@ -343,6 +352,17 @@
     for copy in pos_copies + stat_copies + loss_copies:
         copy.wait_send()
     for copy in stores:
+        copy.wait()
+
+
+def hand_over(sumq_ref, sumd_ref, outq_ref, outd_ref, sem):
+    copies = [
+        pltpu.make_async_copy(sumq_ref, outq_ref, sem.at[0]),
+        pltpu.make_async_copy(sumd_ref, outd_ref, sem.at[1]),
+    ]
+    for copy in copies:
+        copy.start()
+    for copy in copies:
         copy.wait()
 
 
@@ -391,7 +411,7 @@
         ],
         compiler_params=pltpu.CompilerParams(
             collective_id=0, has_side_effects=True,
-            vmem_limit_bytes=56 << 20,
+            vmem_limit_bytes=VMEM_BYTES,
         ),
         cost_estimate=pl.CostEstimate(
             flops=6 * nq * c * nd * c * width,
@@ -399,6 +419,17 @@
             transcendentals=nq * c * nd * c,
         ),
     )(queries, documents, positives.reshape(1, c))
+    grad_q, grad_d = pl.pallas_call(
+        hand_over,
+        out_shape=(tile, tile),
+        in_specs=[anywhere] * 2,
+        out_specs=(anywhere, anywhere),
+        scratch_shapes=[dma((2,))],
+        compiler_params=pltpu.CompilerParams(vmem_limit_bytes=VMEM_BYTES),
+        cost_estimate=pl.CostEstimate(
+            flops=0, bytes_accessed=16 * c * width, transcendentals=0
+        ),
+    )(grad_q, grad_d)
     return (loss.reshape(()), grad_q, grad_d)
 
 

time: 54.9 us -> 76.4 us (1.39)
  Pallas kernels: 49.7 us -> 73.9 us
  local copies, waits for them, and re-layouts: 2.57 us -> 0 us
    pallas_call x0 -> x1, Pallas kernels: none -> 24.9 us  [local(): pl.pallas_call(hand_over, out_shape=(tile, tile), in_specs=[anywhere] * 2...]
    unnamed x4 -> x0, local copies, waits for them, and re-layouts: 2.57 us -> none
    pallas_call x1, Pallas kernels: 49.7 us -> 48.9 us  [local(): pl.pallas_call(functools.partial(kernel, n, qbits, dbits), out_shape=(jax...]
where the time goes in v4:
time: 76.4 us; the launch traced here: 76.3 us
  Pallas kernels  73.9 us (97%)
  between operations  2.41 us (3%)
    pallas_call x1, Pallas kernels, local(): pl.pallas_call(functools.partial(kernel, n, qbits, dbits), out_shape=(jax...  48.9 us
    pallas_call x1, Pallas kernels, local(): pl.pallas_call(hand_over, out_shape=(tile, tile), in_specs=[anywhere] * 2...  24.9 us

profile of v4, /device:TPU:0, one launch (start us, length us, event | category | flops | bytes accessed | tf_op | source)
XLA Modules:
  0.0 76.3 jit_solution(1194002572841004706)
XLA Ops:
  0.6 48.9 %shard_map.58 = (f32[1,1]{1,0:T(1,128)}, f32[128,768]{1,0:T(8,128)}, f32[128,768]{1,0:T(8,128)}) custom-call(bf16[128,768]{1,0:T(8,128)(2,1)} %q_ref.1, bf16[128,768]{1,0:T(8,128)(2,1)} %d_ref.1, s32[1,128]{1,0:T(1,128)} %bitcast.2), custom_call_target="tpu_custom_call" | custom-call | flops 2415919104 | bytes 1179648 | tf_op jit(solution)/shard_map/pallas_call | solution.py:400
  49.6 24.9 %shard_map.59 = (f32[128,768]{1,0:T(8,128)}, f32[128,768]{1,0:T(8,128)}) custom-call(f32[128,768]{1,0:T(8,128)} %get-tuple-element.9.sumq_ref, f32[128,768]{1,0:T(8,128)} %get-tuple-element.10.sumd_ref), custom_call_target="tpu_custom_call" | custom-call | bytes 1572864 | tf_op jit(solution)/shard_map/pallas_call | solution.py:422

commit v5 on v4

--- a/solution.py
+++ b/solution.py
@@ -7,7 +7,7 @@
 from jax.experimental.pallas import tpu as pltpu
 from jax.sharding import PartitionSpec as P
 
-PIECES = 2
+PIECES = 4
 VMEM_BYTES = 56 << 20
 F32 = jnp.float32
 BF16 = jnp.bfloat16
@@ -355,14 +355,24 @@
         copy.wait()
 
 
-def hand_over(sumq_ref, sumd_ref, outq_ref, outd_ref, sem):
-    copies = [
-        pltpu.make_async_copy(sumq_ref, outq_ref, sem.at[0]),
-        pltpu.make_async_copy(sumd_ref, outd_ref, sem.at[1]),
-    ]
-    for copy in copies:
+def hand_over(sumq_ref, sumd_ref, outq_ref, outd_ref, stage, sem):
+    rows = sumq_ref.shape[0] // 2
+    parts = [
+        (ref.at[pl.ds(h * rows, rows), :], out.at[pl.ds(h * rows, rows), :])
+        for ref, out in ((sumq_ref, outq_ref), (sumd_ref, outd_ref)) for h in range(2)
+    ]
+    loads = [
+        pltpu.make_async_copy(ref, stage.at[i], sem.at[0, i]) for i, (ref, out) in enumerate(parts)
+    ]
+    stores = [
+        pltpu.make_async_copy(stage.at[i], out, sem.at[1, i]) for i, (ref, out) in enumerate(parts)
+    ]
+    for copy in loads:
         copy.start()
-    for copy in copies:
+    for load, store in zip(loads, stores):
+        load.wait()
+        store.start()
+    for copy in stores:
         copy.wait()
 
 
@@ -424,7 +434,7 @@
         out_shape=(tile, tile),
         in_specs=[anywhere] * 2,
         out_specs=(anywhere, anywhere),
-        scratch_shapes=[dma((2,))],
+        scratch_shapes=[pltpu.VMEM((4, c // 2, width), F32), dma((2, 4))],
         compiler_params=pltpu.CompilerParams(vmem_limit_bytes=VMEM_BYTES),
         cost_estimate=pl.CostEstimate(
             flops=0, bytes_accessed=16 * c * width, transcendentals=0

time: 76.4 us -> 53.6 us (0.70)
  Pallas kernels: 73.9 us -> 51 us
    pallas_call x1, Pallas kernels: 24.9 us -> 1.97 us  [local(): pl.pallas_call(hand_over, out_shape=(tile, tile), in_specs=[anywhere] * 2...]
where the time goes in v5:
time: 53.6 us; the launch traced here: 53.4 us
  Pallas kernels  51 us (95%)
  between operations  2.41 us (4%)
    pallas_call x1, Pallas kernels, local(): pl.pallas_call(functools.partial(kernel, n, qbits, dbits), out_shape=(jax...  49 us
    pallas_call x1, Pallas kernels, local(): pl.pallas_call(hand_over, out_shape=(tile, tile), in_specs=[anywhere] * 2...  1.97 us

profile of v5, /device:TPU:0, one launch (start us, length us, event | category | flops | bytes accessed | tf_op | source)
XLA Modules:
  0.0 53.4 jit_solution(927275675701368176)
XLA Ops:
  0.6 49.0 %shard_map.58 = (f32[1,1]{1,0:T(1,128)}, f32[128,768]{1,0:T(8,128)}, f32[128,768]{1,0:T(8,128)}) custom-call(bf16[128,768]{1,0:T(8,128)(2,1)} %q_ref.1, bf16[128,768]{1,0:T(8,128)(2,1)} %d_ref.1, s32[1,128]{1,0:T(1,128)} %bitcast.2), custom_call_target="tpu_custom_call" | custom-call | flops 2415919104 | bytes 1179648 | tf_op jit(solution)/shard_map/pallas_call | solution.py:410
  49.7 2.0 %shard_map.59 = (f32[128,768]{1,0:T(8,128)}, f32[128,768]{1,0:T(8,128)}) custom-call(f32[128,768]{1,0:T(8,128)} %get-tuple-element.9.sumq_ref, f32[128,768]{1,0:T(8,128)} %get-tuple-element.10.sumd_ref), custom_call_target="tpu_custom_call" | custom-call | bytes 1572864 | tf_op jit(solution)/shard_map/pallas_call | solution.py:432

commit v6 on v5

--- a/solution.py
+++ b/solution.py
@@ -7,7 +7,7 @@
 from jax.experimental.pallas import tpu as pltpu
 from jax.sharding import PartitionSpec as P
 
-PIECES = 4
+PIECES = 2
 VMEM_BYTES = 56 << 20
 F32 = jnp.float32
 BF16 = jnp.bfloat16
@@ -191,6 +191,13 @@
     ]
     for copy in stat_copies:
         copy.start()
+    for p in range(PIECES):
+        for slot in range(1, nq):
+            gq(slot, p).wait_send()
+        for slot in range(1, nd):
+            gd(slot, p).wait_send()
+    for copy in pos_copies:
+        copy.wait_send()
     for copy in stat_copies:
         copy.wait_recv()
 
@@ -246,13 +253,9 @@
             aqs_sem.at[slot, p], aqr_sem.at[slot, p], peer_q[half],
         )
 
-    def send(which, slot, p):
-        if which == "q" and slot >= half:
-            wide_copy(slot, p).start()
-            return
-        acc, place, code, scale, copies = (
-            (accq, place_q, codeq, scaleq, nq_copies) if which == "q"
-            else (accd, place_d, coded, scaled, nd_copies)
+    def pack(which, slot, p):
+        acc, place, code, scale = (
+            (accq, place_q, codeq, scaleq) if which == "q" else (accd, place_d, coded, scaled)
         )
         value = acc[pl.ds(place(slot) * c + p * piece, piece), :]
         top = jnp.maximum(jnp.max(jnp.abs(value), axis=1, keepdims=True), 1e-30)
@@ -261,32 +264,48 @@
         scale[slot * PIECES + p] = jnp.sum(
             jnp.where(diagonal, top * (1.0 / 32767.0), 0.0), axis=0, keepdims=True
         )
-        for copy in copies(slot, p):
-            copy.start()
+
+    def copies_of(which, slot, p):
+        if which == "q" and slot >= half:
+            return (wide_copy(slot, p),)
+        return nq_copies(slot, p) if which == "q" else nd_copies(slot, p)
+
+    def send(which, slot, pieces=range(PIECES)):
+        if which == "d" or slot < half:
+            for p in pieces:
+                pack(which, slot, p)
+        for p in pieces:
+            for copy in copies_of(which, slot, p):
+                copy.start()
+
+    def add(which, slot, p):
+        into = slot - (1 << stage_of(slot))
+        if which == "q" and slot >= half:
+            value = wideq[pl.ds((slot - half) * c + p * piece, piece), :]
+        else:
+            got, gots = (gotq, gotsq) if which == "q" else (gotd, gotsd)
+            scales = jnp.sum(
+                jnp.where(diagonal, gots[slot * PIECES + p], 0.0), axis=1, keepdims=True
+            )
+            codes = got[pl.ds(slot * c + p * piece, piece), :]
+            value = codes.astype(jnp.int32).astype(F32) * scales
+        acc, place = (accq, place_q) if which == "q" else (accd, place_d)
+        rows = pl.ds(place(into) * c + p * piece, piece)
+        acc[rows, :] = acc[rows, :] + value
 
     def absorb(which, slots):
         for slot in slots:
             into = slot - (1 << stage_of(slot))
-            for p in range(PIECES):
-                if which == "q" and slot >= half:
-                    wide_copy(slot, p).wait_recv()
-                    value = wideq[pl.ds((slot - half) * c + p * piece, piece), :]
-                else:
-                    got, gots, copies = (
-                        (gotq, gotsq, nq_copies) if which == "q" else (gotd, gotsd, nd_copies)
-                    )
-                    for copy in copies(slot, p):
+            onward = into > 0 and stage_of(slot) == stage_of(into) + 1
+            groups = [[p] for p in range(PIECES)] if onward else [range(PIECES)]
+            for pieces in groups:
+                for p in pieces:
+                    for copy in copies_of(which, slot, p):
                         copy.wait_recv()
-                    scales = jnp.sum(
-                        jnp.where(diagonal, gots[slot * PIECES + p], 0.0), axis=1, keepdims=True
-                    )
-                    codes = got[pl.ds(slot * c + p * piece, piece), :]
-                    value = codes.astype(jnp.int32).astype(F32) * scales
-                acc, place = (accq, place_q) if which == "q" else (accd, place_d)
-                rows = pl.ds(place(into) * c + p * piece, piece)
-                acc[rows, :] = acc[rows, :] + value
-                if into and stage_of(slot) == stage_of(into) + 1:
-                    send(which, into, p)
+                for p in pieces:
+                    add(which, slot, p)
+                if onward:
+                    send(which, into, pieces)
 
     def grad_q(slots):
         for slot in slots:
@@ -294,15 +313,13 @@
             accq[rows, :] = lax.dot_general(
                 wts[:, rows], dall[...], (((0,), (0,)), ((), ())), preferred_element_type=F32
             )
-            for p in range(PIECES):
-                send("q", slot + half, p)
+            send("q", slot + half)
 
     def grad_d(slots):
         for slot in slots:
             rows = pl.ds(place_d(slot) * c, pair)
             accd[rows, :] = jnp.dot(wts[rows, :], qall[...], preferred_element_type=F32)
-            for p in range(PIECES):
-                send("d", slot + nd // 2, p)
+            send("d", slot + nd // 2)
 
     early_q, late_q = falling(half, half // 2), falling(half // 2, 0)
     for slot in falling(nd // 2, nd // 4):
@@ -313,13 +330,18 @@
     grad_q(early_q)
     absorb("q", [early_q[0] + half])
     grad_d(falling(nd // 4, 0))
+    absorb("d", falling(nd, 3 * nd // 4))
     absorb("q", [slot + half for slot in early_q[1:]])
     grad_q(late_q)
     for copy in loss_copies:
         copy.start()
 
-    absorb("d", falling(nd, 3 * nd // 4))
     absorb("q", [slot + half for slot in late_q])
+    for p in range(PIECES):
+        for slot in range(half, nq):
+            wide_copy(slot, p).wait_send()
+    for copy in stat_copies:
+        copy.wait_send()
     rest_q, rest_d = falling(half, 1), falling(3 * nd // 4, 1)
     for i in range(max(len(rest_q), len(rest_d))):
         absorb("q", rest_q[i:i + 1])
@@ -341,15 +363,13 @@
     loss_ref[...] = jnp.sum(row, axis=1, keepdims=True) / (c * n)
 
     for p in range(PIECES):
-        for slot in range(1, nq):
-            gq(slot, p).wait_send()
-            for copy in nq_copies(slot, p) if slot < half else (wide_copy(slot, p),):
+        for slot in range(1, half):
+            for copy in nq_copies(slot, p):
                 copy.wait_send()
         for slot in range(1, nd):
-            gd(slot, p).wait_send()
             for copy in nd_copies(slot, p):
                 copy.wait_send()
-    for copy in pos_copies + stat_copies + loss_copies:
+    for copy in loss_copies:
         copy.wait_send()
     for copy in stores:
         copy.wait()

time: 53.6 us -> 54.7 us (1.021)
  Pallas kernels: 51 us -> 52.2 us
    pallas_call x1, Pallas kernels: 49 us -> 50.2 us  [local(): pl.pallas_call(functools.partial(kernel, n, qbits, dbits), out_shape=(jax...]
where the time goes in v6:
time: 54.7 us; the launch traced here: 54.6 us
  Pallas kernels  52.2 us (95%)
  between operations  2.41 us (4%)
    pallas_call x1, Pallas kernels, local(): pl.pallas_call(functools.partial(kernel, n, qbits, dbits), out_shape=(jax...  50.2 us
    pallas_call x1, Pallas kernels, local(): pl.pallas_call(hand_over, out_shape=(tile, tile), in_specs=[anywhere] * 2...  1.97 us

profile of v6, /device:TPU:0, one launch (start us, length us, event | category | flops | bytes accessed | tf_op | source)
XLA Modules:
  0.0 54.6 jit_solution(12993213230970292651)
XLA Ops:
  0.6 50.2 %shard_map.58 = (f32[1,1]{1,0:T(1,128)}, f32[128,768]{1,0:T(8,128)}, f32[128,768]{1,0:T(8,128)}) custom-call(bf16[128,768]{1,0:T(8,128)(2,1)} %q_ref.1, bf16[128,768]{1,0:T(8,128)(2,1)} %d_ref.1, s32[1,128]{1,0:T(1,128)} %bitcast.2), custom_call_target="tpu_custom_call" | custom-call | flops 2415919104 | bytes 1179648 | tf_op jit(solution)/shard_map/pallas_call | solution.py:430
  50.8 2.0 %shard_map.59 = (f32[128,768]{1,0:T(8,128)}, f32[128,768]{1,0:T(8,128)}) custom-call(f32[128,768]{1,0:T(8,128)} %get-tuple-element.9.sumq_ref, f32[128,768]{1,0:T(8,128)} %get-tuple-element.10.sumd_ref), custom_call_target="tpu_custom_call" | custom-call | bytes 1572864 | tf_op jit(solution)/shard_map/pallas_call | solution.py:452

commit v7 on v5

--- a/solution.py
+++ b/solution.py
@@ -7,7 +7,8 @@
 from jax.experimental.pallas import tpu as pltpu
 from jax.sharding import PartitionSpec as P
 
-PIECES = 4
+PIECES = 2
+SHARD_PIECES = 4
 VMEM_BYTES = 56 << 20
 F32 = jnp.float32
 BF16 = jnp.bfloat16
@@ -59,7 +60,7 @@
 ):
     me = lax.axis_index("dp")
     c, width = q_ref.shape
-    piece = c // PIECES
+    piece, part = c // PIECES, c // SHARD_PIECES
     nq, nd = 1 << len(qbits), 1 << len(dbits)
     half = nq // 2
 
@@ -106,8 +107,8 @@
     def gather_copy(buf, place, send, recv, peers, slot, p):
         low = slot - (1 << stage_of(slot))
         return remote(
-            buf.at[pl.ds(place(low) * c + p * piece, piece), :],
-            buf.at[pl.ds(place(slot) * c + p * piece, piece), :],
+            buf.at[pl.ds(place(low) * c + p * part, part), :],
+            buf.at[pl.ds(place(slot) * c + p * part, part), :],
             send.at[slot, p], recv.at[slot, p], peers[1 << stage_of(slot)],
         )
 
@@ -119,7 +120,7 @@
         for k in range(1, nq)
     ]
 
-    for p in range(PIECES):
+    for p in range(SHARD_PIECES):
         for j in range(len(qbits)):
             gq(1 << j, p).start()
             if j < len(dbits):
@@ -129,7 +130,7 @@
 
     def arrive(make, bits, slots):
         for slot in slots:
-            for p in range(PIECES):
+            for p in range(SHARD_PIECES):
                 make(slot, p).wait_recv()
                 for j in range(stage_of(slot) + 1, len(bits)):
                     make(slot + (1 << j), p).start()
@@ -340,13 +341,16 @@
     row = tree_sum([losses[k] for k in range(nd)])
     loss_ref[...] = jnp.sum(row, axis=1, keepdims=True) / (c * n)
 
+    for p in range(SHARD_PIECES):
+        for slot in range(1, nq):
+            gq(slot, p).wait_send()
+        for slot in range(1, nd):
+            gd(slot, p).wait_send()
     for p in range(PIECES):
         for slot in range(1, nq):
-            gq(slot, p).wait_send()
             for copy in nq_copies(slot, p) if slot < half else (wide_copy(slot, p),):
                 copy.wait_send()
         for slot in range(1, nd):
-            gd(slot, p).wait_send()
             for copy in nd_copies(slot, p):
                 copy.wait_send()
     for copy in pos_copies + stat_copies + loss_copies:
@@ -413,7 +417,8 @@
         in_specs=[anywhere] * 3,
         out_specs=(vmem, anywhere, anywhere),
         scratch_shapes=[pltpu.VMEM(shape, kind) for shape, kind in buffers] + [
-            dma((nq, PIECES)), dma((nq, PIECES)), dma((nd, PIECES)), dma((nd, PIECES)),
+            dma((nq, SHARD_PIECES)), dma((nq, SHARD_PIECES)),
+            dma((nd, SHARD_PIECES)), dma((nd, SHARD_PIECES)),
             dma((nq,)), dma((nq,)), dma((nq,)), dma((nq,)), dma((nd,)), dma((nd,)),
             dma((nq, PIECES)), dma((nq, PIECES)), dma((nd, PIECES)), dma((nd, PIECES)),
             dma((nq, PIECES)), dma((nq, PIECES)), dma((nd, PIECES)), dma((nd, PIECES)),

time: 53.6 us -> 53 us (0.989)
  Pallas kernels: 51 us -> 50.4 us
    pallas_call x1, Pallas kernels: 49 us -> 48.4 us  [local(): pl.pallas_call(functools.partial(kernel, n, qbits, dbits), out_shape=(jax...]
where the time goes in v7:
time: 53 us; the launch traced here: 52.8 us
  Pallas kernels  50.4 us (95%)
  between operations  2.41 us (5%)
    pallas_call x1, Pallas kernels, local(): pl.pallas_call(functools.partial(kernel, n, qbits, dbits), out_shape=(jax...  48.4 us
    pallas_call x1, Pallas kernels, local(): pl.pallas_call(hand_over, out_shape=(tile, tile), in_specs=[anywhere] * 2...  1.97 us

profile of v7, /device:TPU:0, one launch (start us, length us, event | category | flops | bytes accessed | tf_op | source)
XLA Modules:
  0.0 52.8 jit_solution(7933243060629725188)
XLA Ops:
  0.6 48.4 %shard_map.58 = (f32[1,1]{1,0:T(1,128)}, f32[128,768]{1,0:T(8,128)}, f32[128,768]{1,0:T(8,128)}) custom-call(bf16[128,768]{1,0:T(8,128)(2,1)} %q_ref.1, bf16[128,768]{1,0:T(8,128)(2,1)} %d_ref.1, s32[1,128]{1,0:T(1,128)} %bitcast.2), custom_call_target="tpu_custom_call" | custom-call | flops 2415919104 | bytes 1179648 | tf_op jit(solution)/shard_map/pallas_call | solution.py:414
  49.1 2.0 %shard_map.59 = (f32[128,768]{1,0:T(8,128)}, f32[128,768]{1,0:T(8,128)}) custom-call(f32[128,768]{1,0:T(8,128)} %get-tuple-element.9.sumq_ref, f32[128,768]{1,0:T(8,128)} %get-tuple-element.10.sumd_ref), custom_call_target="tpu_custom_call" | custom-call | bytes 1572864 | tf_op jit(solution)/shard_map/pallas_call | solution.py:437

commit v8 on v7

--- a/solution.py
+++ b/solution.py
@@ -321,31 +321,37 @@
 
     absorb("d", falling(nd, 3 * nd // 4))
     absorb("q", [slot + half for slot in late_q])
-    rest_q, rest_d = falling(half, 1), falling(3 * nd // 4, 1)
-    for i in range(max(len(rest_q), len(rest_d))):
-        absorb("q", rest_q[i:i + 1])
-        absorb("d", rest_d[i:i + 1])
-
-    own = pl.ds(0, c)
-    stores = [
-        pltpu.make_async_copy(accq.at[own, :], outq_ref, io_sem.at[3]),
-        pltpu.make_async_copy(accd.at[own, :], outd_ref, io_sem.at[4]),
-    ]
-    accq[own, :] = project(20.0 * accq[own, :], *normalize(qown[...]))
-    stores[0].start()
-    accd[own, :] = project(20.0 * accd[own, :], *normalize(down[...]))
-    stores[1].start()
-
-    for copy in loss_copies:
-        copy.wait_recv()
-    row = tree_sum([losses[k] for k in range(nd)])
-    loss_ref[...] = jnp.sum(row, axis=1, keepdims=True) / (c * n)
-
+    rest_q, rest_d = falling(half, 2), falling(3 * nd // 4, 1)
+    absorb("q", rest_q[:1])
+    absorb("d", rest_d[:1])
     for p in range(SHARD_PIECES):
         for slot in range(1, nq):
             gq(slot, p).wait_send()
         for slot in range(1, nd):
             gd(slot, p).wait_send()
+    for copy in pos_copies + stat_copies:
+        copy.wait_send()
+    for i in range(1, max(len(rest_q), len(rest_d))):
+        absorb("q", rest_q[i:i + 1])
+        absorb("d", rest_d[i:min(i + 1, len(rest_d) - 1)])
+    absorb("q", [1])
+
+    own = pl.ds(0, c)
+    stores = [
+        pltpu.make_async_copy(accq.at[own, :], outq_ref, io_sem.at[3]),
+        pltpu.make_async_copy(accd.at[own, :], outd_ref, io_sem.at[4]),
+    ]
+    accq[own, :] = project(20.0 * accq[own, :], *normalize(qown[...]))
+    stores[0].start()
+    absorb("d", [1])
+    accd[own, :] = project(20.0 * accd[own, :], *normalize(down[...]))
+    stores[1].start()
+
+    for copy in loss_copies:
+        copy.wait_recv()
+    row = tree_sum([losses[k] for k in range(nd)])
+    loss_ref[...] = jnp.sum(row, axis=1, keepdims=True) / (c * n)
+
     for p in range(PIECES):
         for slot in range(1, nq):
             for copy in nq_copies(slot, p) if slot < half else (wide_copy(slot, p),):
@@ -353,7 +359,7 @@
         for slot in range(1, nd):
             for copy in nd_copies(slot, p):
                 copy.wait_send()
-    for copy in pos_copies + stat_copies + loss_copies:
+    for copy in loss_copies:
         copy.wait_send()
     for copy in stores:
         copy.wait()

time: 53 us -> 53.2 us (level)
  no operation moved by 1% of the time
where the time goes in v8:
time: 53.2 us; the launch traced here: 53 us
  Pallas kernels  50.6 us (95%)
  between operations  2.41 us (5%)
    pallas_call x1, Pallas kernels, local(): pl.pallas_call(functools.partial(kernel, n, qbits, dbits), out_shape=(jax...  48.6 us
    pallas_call x1, Pallas kernels, local(): pl.pallas_call(hand_over, out_shape=(tile, tile), in_specs=[anywhere] * 2...  1.97 us

profile of v8, /device:TPU:0, one launch (start us, length us, event | category | flops | bytes accessed | tf_op | source)
XLA Modules:
  0.0 53.0 jit_solution(14479434638719886020)
XLA Ops:
  0.6 48.6 %shard_map.58 = (f32[1,1]{1,0:T(1,128)}, f32[128,768]{1,0:T(8,128)}, f32[128,768]{1,0:T(8,128)}) custom-call(bf16[128,768]{1,0:T(8,128)(2,1)} %q_ref.1, bf16[128,768]{1,0:T(8,128)(2,1)} %d_ref.1, s32[1,128]{1,0:T(1,128)} %bitcast.2), custom_call_target="tpu_custom_call" | custom-call | flops 2415919104 | bytes 1179648 | tf_op jit(solution)/shard_map/pallas_call | solution.py:420
  49.2 2.0 %shard_map.59 = (f32[128,768]{1,0:T(8,128)}, f32[128,768]{1,0:T(8,128)}) custom-call(f32[128,768]{1,0:T(8,128)} %get-tuple-element.9.sumq_ref, f32[128,768]{1,0:T(8,128)} %get-tuple-element.10.sumd_ref), custom_call_target="tpu_custom_call" | custom-call | bytes 1572864 | tf_op jit(solution)/shard_map/pallas_call | solution.py:443

commit v9 on v7

--- a/solution.py
+++ b/solution.py
@@ -201,7 +201,6 @@
         )
 
     totals = [slot_total(0, r) for r in range(nq)]
-    losses[0] = tree_sum([20.0 + jnp.log(totals[r]) - slot_total(1, r) for r in range(nq)])
     loss_copies = [
         remote(losses.at[0], losses.at[k], ls_sem.at[k], lr_sem.at[k], peer_d[k])
         for k in range(1, nd)
@@ -316,6 +315,7 @@
     grad_d(falling(nd // 4, 0))
     absorb("q", [slot + half for slot in early_q[1:]])
     grad_q(late_q)
+    losses[0] = tree_sum([20.0 + jnp.log(totals[r]) - slot_total(1, r) for r in range(nq)])
     for copy in loss_copies:
         copy.start()
 

time: 53 us -> 53 us (level)
  no operation moved by 1% of the time
where the time goes in v9:
time: 53 us; the launch traced here: 52.8 us
  Pallas kernels  50.4 us (95%)
  between operations  2.41 us (5%)
    pallas_call x1, Pallas kernels, local(): pl.pallas_call(functools.partial(kernel, n, qbits, dbits), out_shape=(jax...  48.4 us
    pallas_call x1, Pallas kernels, local(): pl.pallas_call(hand_over, out_shape=(tile, tile), in_specs=[anywhere] * 2...  1.97 us

profile of v9, /device:TPU:0, one launch (start us, length us, event | category | flops | bytes accessed | tf_op | source)
XLA Modules:
  0.0 52.8 jit_solution(3806191430075815678)
XLA Ops:
  0.6 48.4 %shard_map.58 = (f32[1,1]{1,0:T(1,128)}, f32[128,768]{1,0:T(8,128)}, f32[128,768]{1,0:T(8,128)}) custom-call(bf16[128,768]{1,0:T(8,128)(2,1)} %q_ref.1, bf16[128,768]{1,0:T(8,128)(2,1)} %d_ref.1, s32[1,128]{1,0:T(1,128)} %bitcast.2), custom_call_target="tpu_custom_call" | custom-call | flops 2415919104 | bytes 1179648 | tf_op jit(solution)/shard_map/pallas_call | solution.py:414
  49.1 2.0 %shard_map.59 = (f32[128,768]{1,0:T(8,128)}, f32[128,768]{1,0:T(8,128)}) custom-call(f32[128,768]{1,0:T(8,128)} %get-tuple-element.9.sumq_ref, f32[128,768]{1,0:T(8,128)} %get-tuple-element.10.sumd_ref), custom_call_target="tpu_custom_call" | custom-call | bytes 1572864 | tf_op jit(solution)/shard_map/pallas_call | solution.py:437
